TPU v7x, 32 devices: a whole 2x2x4 slice. The times are simulated.
32 devices in a mesh: groups: 2 (over x), mp: 16 (over z, y, core).
Axes of the slice: x: 2, y: 2, z: 4, core: 2. Of those that a mesh axis runs over, the one named last changes fastest.
Arguments:
- features: bfloat16 [32, 256, 128, 128], P(None, ('groups', 'mp')), parts along dimension 1, may hold values from -6 to 6
- cotangent: bfloat16 [32, 256, 128, 128], P(None, ('groups', 'mp')), parts along dimension 1, may hold values from -9 to 9
- spectral_weight: float32 [256, 2, 16, 32, 32], P('mp'), may hold values from -9 to 9
- pointwise_weight: bfloat16 [32, 32], replicated, may hold values from -1 to 1
- biases: float32 [32], replicated, may hold values from -3 to 3
Outputs:
- features_grad: bfloat16 [32, 256, 128, 128], P(None, ('groups', 'mp')), parts along dimension 1
- spectral_grad: float32 [512, 2, 16, 32, 32], P(('groups', 'mp')), parts along dimension 0
- pointwise_grad: float32 [64, 32], P('groups'), parts along dimension 0
- biases_grad: float32 [64], P('groups'), parts along dimension 0
There are 2 independent parts, one for each index of `groups`. A program takes and returns all parts, laid end to end along the dimension named above; an argument that names none is the same for every part. Nothing has to cross between parts.
All inputs are finite; a program needn't handle non-finite values.
Results may differ from a plain program's by a relative error of at most 0.007.
Values sent between devices are 32-bit elements; how exact they have to be, the bound alone decides.
A program may use at most 128 MiB of HBM per device.

v0:
```python
import math

import jax
import jax.numpy as jnp
from jax import lax
from jax.sharding import PartitionSpec as P

NX = 128
NY = 128
NZ = 128
KX = 16
KY = 16
KZ = 16


precise = lax.Precision.HIGHEST


def axis_tables(length, mode_count, signed):
    freqs = jnp.arange(mode_count, dtype=jnp.int32) - (mode_count // 2 if signed else 0)
    spots = jnp.arange(length, dtype=jnp.int32)
    phases = (spots[:, None] * freqs[None, :] % length).astype(jnp.float32) * (
        2.0 * math.pi / length
    )
    return (jnp.cos(phases), jnp.sin(phases))


def spectrum_plane(data, z_cos, z_sin, y_cos, y_sin, z_scale):
    z_real = (
        jnp.einsum("cxyz,zk->kcxy", data, z_cos, preferred_element_type=jnp.float32)
        * z_scale[:, None, None, None]
    )
    z_imag = (
        -jnp.einsum("cxyz,zk->kcxy", data, z_sin, preferred_element_type=jnp.float32)
        * z_scale[:, None, None, None]
    )
    y_real = jnp.einsum("kcxy,yj->jkcx", z_real, y_cos, precision=precise) + jnp.einsum(
        "kcxy,yj->jkcx", z_imag, y_sin, precision=precise
    )
    y_imag = jnp.einsum("kcxy,yj->jkcx", z_imag, y_cos, precision=precise) - jnp.einsum(
        "kcxy,yj->jkcx", z_real, y_sin, precision=precise
    )
    stacked = jnp.stack([y_real, y_imag], axis=2)
    return stacked.reshape(KY * KZ, 2, stacked.shape[3], stacked.shape[4])


def spectrum_lines(part, x_cos, x_sin):
    a_real = part[:, 0]
    a_imag = part[:, 1]
    v_real = jnp.einsum("pcx,xk->pck", a_real, x_cos, precision=precise) + jnp.einsum(
        "pcx,xk->pck", a_imag, x_sin, precision=precise
    )
    v_imag = jnp.einsum("pcx,xk->pck", a_imag, x_cos, precision=precise) - jnp.einsum(
        "pcx,xk->pck", a_real, x_sin, precision=precise
    )
    return jnp.stack([v_real, v_imag], axis=1)


def space_lines(spec, x_cos, x_sin):
    u_real = spec[:, 0]
    u_imag = spec[:, 1]
    b_real = jnp.einsum("pck,xk->pcx", u_real, x_cos, precision=precise) - jnp.einsum(
        "pck,xk->pcx", u_imag, x_sin, precision=precise
    )
    b_imag = jnp.einsum("pck,xk->pcx", u_imag, x_cos, precision=precise) + jnp.einsum(
        "pck,xk->pcx", u_real, x_sin, precision=precise
    )
    return jnp.stack([b_real, b_imag], axis=1)


def space_plane(stacked, y_cos, y_sin, z_cos, z_sin):
    grid = stacked.reshape(KY, KZ, 2, stacked.shape[2], stacked.shape[3])
    q_real = grid[:, :, 0]
    q_imag = grid[:, :, 1]
    b_real = jnp.einsum("jkcx,yj->kcxy", q_real, y_cos, precision=precise) - jnp.einsum(
        "jkcx,yj->kcxy", q_imag, y_sin, precision=precise
    )
    b_imag = jnp.einsum("jkcx,yj->kcxy", q_imag, y_cos, precision=precise) + jnp.einsum(
        "jkcx,yj->kcxy", q_real, y_sin, precision=precise
    )
    return jnp.einsum("kcxy,zk->cxyz", b_real, z_cos, precision=precise) - jnp.einsum(
        "kcxy,zk->cxyz", b_imag, z_sin, precision=precise
    )


def modes_product(spec, weight):
    v_real, v_imag = (spec[:, 0], spec[:, 1])
    r_real, r_imag = (weight[:, 0], weight[:, 1])
    u_real = jnp.einsum("pck,pkco->pok", v_real, r_real, precision=precise) - jnp.einsum(
        "pck,pkco->pok", v_imag, r_imag, precision=precise
    )
    u_imag = jnp.einsum("pck,pkco->pok", v_real, r_imag, precision=precise) + jnp.einsum(
        "pck,pkco->pok", v_imag, r_real, precision=precise
    )
    return jnp.stack([u_real, u_imag], axis=1)


def modes_adjoint(dspec, weight):
    d_real, d_imag = (dspec[:, 0], dspec[:, 1])
    r_real, r_imag = (weight[:, 0], weight[:, 1])
    g_real = jnp.einsum("pok,pkco->pck", d_real, r_real, precision=precise) + jnp.einsum(
        "pok,pkco->pck", d_imag, r_imag, precision=precise
    )
    g_imag = jnp.einsum("pok,pkco->pck", d_imag, r_real, precision=precise) - jnp.einsum(
        "pok,pkco->pck", d_real, r_imag, precision=precise
    )
    return jnp.stack([g_real, g_imag], axis=1)


def modes_gradient(spec, dspec):
    v_real, v_imag = (spec[:, 0], spec[:, 1])
    d_real, d_imag = (dspec[:, 0], dspec[:, 1])
    w_real = jnp.einsum("pck,pok->pkco", v_real, d_real, precision=precise) + jnp.einsum(
        "pck,pok->pkco", v_imag, d_imag, precision=precise
    )
    w_imag = jnp.einsum("pck,pok->pkco", v_real, d_imag, precision=precise) - jnp.einsum(
        "pck,pok->pkco", v_imag, d_real, precision=precise
    )
    return jnp.stack([w_real, w_imag], axis=1)


def to_modes(partial_value, x_cos_mine, x_sin_mine):
    return lax.psum_scatter(
        spectrum_lines(partial_value, x_cos_mine, x_sin_mine), "mp", scatter_dimension=0, tiled=True
    )


def to_space(spec, x_cos_mine, x_sin_mine):
    return space_lines(lax.all_gather(spec, "mp", axis=0, tiled=True), x_cos_mine, x_sin_mine)


def shards(features, cotangent, spectral_weight, pointwise_weight, biases):
    blocks = lax.axis_size("mp")
    rows_mine = NX // blocks
    first_cell = lax.axis_index("mp") * rows_mine
    z_cos, z_sin = axis_tables(NZ, KZ, False)
    z_cos_low = z_cos.astype(jnp.bfloat16)
    z_sin_low = z_sin.astype(jnp.bfloat16)
    y_cos, y_sin = axis_tables(NY, KY, True)
    x_cos, x_sin = axis_tables(NX, KX, True)
    x_cos_mine = lax.dynamic_slice_in_dim(x_cos, first_cell, rows_mine, 0)
    x_sin_mine = lax.dynamic_slice_in_dim(x_sin, first_cell, rows_mine, 0)
    z_weight = jnp.where(jnp.arange(KZ) == 0, 1.0, 2.0).astype(jnp.float32) / float(NX * NY * NZ)
    unit_weight = jnp.ones((KZ,), jnp.float32)
    partial_value = spectrum_plane(features, z_cos_low, z_sin_low, y_cos, y_sin, unit_weight)
    spec = to_modes(partial_value, x_cos_mine, x_sin_mine)
    mixed = modes_product(spec, spectral_weight)
    spectral = space_plane(
        to_space(mixed, x_cos_mine, x_sin_mine),
        y_cos,
        y_sin,
        z_cos * z_weight[None, :],
        z_sin * z_weight[None, :],
    )
    local_mix = jnp.einsum(
        "oc,cxyz->oxyz", pointwise_weight, features, preferred_element_type=jnp.float32
    )
    preact = spectral + local_mix + biases[:, None, None, None]
    _, pullback = jax.vjp(jax.nn.gelu, preact)
    pre_grad = pullback(cotangent.astype(jnp.float32))[0].astype(jnp.bfloat16)
    dpartial = spectrum_plane(pre_grad, z_cos_low, z_sin_low, y_cos, y_sin, z_weight)
    dspec = to_modes(dpartial, x_cos_mine, x_sin_mine)
    spectral_grad = modes_gradient(spec, dspec)
    dmixed = modes_adjoint(dspec, spectral_weight)
    back = space_plane(to_space(dmixed, x_cos_mine, x_sin_mine), y_cos, y_sin, z_cos, z_sin)
    local_back = jnp.einsum(
        "oc,oxyz->cxyz", pointwise_weight, pre_grad, preferred_element_type=jnp.float32
    )
    features_grad = (back + local_back).astype(jnp.bfloat16)
    factor = float(NX * NY * NZ) ** (-0.5)
    mix_local = jnp.einsum("oxyz,cxyz->oc", pre_grad, features, preferred_element_type=jnp.float32)
    bias_local = jnp.sum(pre_grad, axis=(1, 2, 3), dtype=jnp.float32)
    mix_total, bias_total = lax.psum((mix_local, bias_local), "mp")
    return (features_grad, spectral_grad, mix_total * factor, bias_total * factor)


def solution(mesh):
    return jax.shard_map(
        shards,
        mesh=mesh,
        in_specs=(
            P(None, ("groups", "mp"), None, None),
            P(None, ("groups", "mp"), None, None),
            P("mp", None, None, None, None),
            P(),
            P(),
        ),
        out_specs=(
            P(None, ("groups", "mp"), None, None),
            P(("groups", "mp"), None, None, None, None),
            P("groups", None),
            P("groups"),
        ),
        check_vma=False,
    )
```

profile of v0, /device:TPU:15, one launch (start us, length us, event | category | flops | bytes accessed | tf_op | source)
XLA Modules:
  0.0 623.7 jit_solution(12048591459338722951)
XLA Ops:
  7.3 5.8 fusion.165
  13.1 2.3 convolution_negate_fusion
  15.6 8.9 %fusion.57 = f32[16,16,32,8]{2,0,3,1:T(8,128)S(1)} fusion(f32[16,32,8,128]{3,0,2,1:T(8,128)S(1)} %convolution_negate_fusion, s32[16]{0:T(128)S(1)} %iota_add_fusion), kind=kOutput, calls=%fused_computation.68 | convolution fusion | flops 100691968 | bytes 2359360 | tf_op jit(solution)/shard_map/kcxy,yj->jkcx/dot_general | solution.py:40
  24.4 10.1 %fusion.59 = f32[16,16,32,8]{2,0,3,1:T(8,128)} fusion(f32[16,32,8,128]{3,0,2,1:T(8,128)S(1)} %convolution_negate_fusion, s32[16]{0:T(128)S(1)} %iota_add_fusion), kind=kOutput, calls=%fused_computation.70 | convolution fusion | flops 100691968 | bytes 2359360 | tf_op jit(solution)/shard_map/kcxy,yj->jkcx/dot_general | solution.py:37
  34.5 11.1 %fusion.65 = f32[16,16,32,8]{2,0,3,1:T(8,128)} fusion(f32[16,16,32,8]{2,0,3,1:T(8,128)} %fusion.59, f32[16,32,8,128]{3,0,2,1:T(8,128)S(1)} %fusion.165, s32[16]{0:T(128)S(1)} %iota_add_fusion), kind=kOutput, calls=%fused_computation.78 | convolution fusion | flops 100757504 | bytes 2621504 | tf_op jit(solution)/shard_map/kcxy,yj->jkcx/dot_general | solution.py:37
  45.6 20.3 %fusion.68 = f32[16,16,32,8]{2,0,3,1:T(8,128)S(1)} fusion(f32[16,16,32,8]{2,0,3,1:T(8,128)S(1)} %fusion.57, f32[16,32,8,128]{3,0,2,1:T(8,128)S(1)} %fusion.165, s32[16]{0:T(128)S(1)} %iota_add_fusion), kind=kOutput, calls=%fused_computation.79 | convolution fusion | flops 100757504 | bytes 2621504 | tf_op jit(solution)/shard_map/kcxy,yj->jkcx/dot_general | solution.py:40
  71.2 4.4 copy.181
  75.7 71.8 %reduce-scatter.3.cloned.1.call-done = f32[16,2,32,16]{2,3,1,0:T(8,128)} async-done(((f32[256,2,32,16]{2,3,1,0:T(8,128)}), f32[16,2,32,16]{2,3,1,0:T(8,128)}) %reduce-scatter.3.cloned.1.call-update) | async-done | bytes 65552 | tf_op jit(solution)/shard_map/reduce_scatter | solution.py:123
  149.2 5.1 fusion.31
  154.4 5.2 fusion.25
  159.6 5.2 fusion.23
  164.7 5.2 fusion.33
  171.2 14.1 %fusion.17 = f32[32,8,128,128]{3,0,2,1:T(8,128)} fusion(bf16[32,8,128,128]{3,2,1,0:T(8,128)(2,1)} %param.5, bf16[32,32]{1,0:T(8,128)(2,1)S(1)} %copy-done), kind=kOutput, calls=%fused_computation.25 | convolution fusion | flops 268435456 | bytes 25167872 | tf_op jit(solution)/shard_map/oc,cxyz->oxyz/dot_general | solution.py:155
  185.3 36.7 %all-gather.3.cloned.1.call-done = f32[256,2,32,16]{2,3,1,0:T(8,128)} async-done(((f32[16,2,32,16]{2,3,1,0:T(8,128)}), f32[256,2,32,16]{2,3,1,0:T(8,128)}) %all-gather.3.cloned.1.call-update) | async-done | bytes 1048592 | tf_op jit(solution)/shard_map/all_gather | solution.py:129
  222.0 3.9 fusion.329
  225.9 2.7 copy.286
  232.6 2.9 copy.187
  235.6 3.4 fusion.124
  239.0 3.2 fusion.150
  248.9 28.8 %fusion.47 = f32[32,8,128,128]{3,2,1,0:T(8,128)} fusion(f32[16,32,8,128]{3,0,2,1:T(8,128)S(1)} %copy-done.4, f32[16,32,8,128]{3,0,2,1:T(8,128)S(1)} %fusion.126, f32[16]{0:T(128)S(1)} %fusion.215), kind=kOutput, calls=%fused_computation.58 | convolution fusion | flops 805861376 | bytes 20971584 | tf_op jit(solution)/shard_map/kcxy,zk->cxyz/dot_general | solution.py:81
  277.7 43.8 %convert_reduce_fusion = (f32[32]{0:T(128)S(1)}, bf16[32,8,128,128]{3,2,1,0:T(8,128)(2,1)S(1)}) fusion(f32[32]{0:T(128)S(1)} %copy-done.9, f32[32,8,128,128]{3,0,2,1:T(8,128)} %fusion.17, f32[32,8,128,128]{3,2,1,0:T(8,128)} %fusion.47, f32[16]{0:T(128)S(1)} %fusion.215, f32[16,32,8,128]{3,0,2,1:T(8,128)S(1)} %fusion.148, ...), kind=kOutput, calls=%fused_computation.18 | convolution fusion | flops 914913280 | bytes 54526272 | tf_op jit(solution)/shard_map/kcxy,zk->cxyz/dot_general | solution.py:81
  321.6 2.3 negate_multiply_fusion
  323.9 8.9 %fusion.49 = f32[16,16,32,8]{2,0,3,1:T(8,128)S(1)} fusion(f32[16,32,8,128]{3,0,2,1:T(8,128)S(1)} %negate_multiply_fusion, s32[16]{0:T(128)S(1)} %iota_add_fusion), kind=kOutput, calls=%fused_computation.60 | convolution fusion | flops 100691968 | bytes 2359360 | tf_op jit(solution)/shard_map/kcxy,yj->jkcx/dot_general | solution.py:40
  332.8 9.1 %fusion.51 = f32[16,16,32,8]{2,0,3,1:T(8,128)S(1)} fusion(f32[16,32,8,128]{3,0,2,1:T(8,128)S(1)} %negate_multiply_fusion, s32[16]{0:T(128)S(1)} %iota_add_fusion), kind=kOutput, calls=%fused_computation.62 | convolution fusion | flops 100691968 | bytes 2359360 | tf_op jit(solution)/shard_map/kcxy,yj->jkcx/dot_general | solution.py:37
  341.9 2.3 convolution_multiply_fusion
  344.2 8.9 %fusion.74 = f32[16,16,32,8]{2,0,3,1:T(8,128)S(1)} fusion(f32[16,16,32,8]{2,0,3,1:T(8,128)S(1)} %fusion.49, f32[16,32,8,128]{3,0,2,1:T(8,128)S(1)} %convolution_multiply_fusion, s32[16]{0:T(128)S(1)} %iota_add_fusion), kind=kOutput, calls=%fused_computation.81 | convolution fusion | flops 100757504 | bytes 2621504 | tf_op jit(solution)/shard_map/kcxy,yj->jkcx/dot_general | solution.py:40
  353.1 9.3 %fusion.71 = f32[16,16,32,8]{2,0,3,1:T(8,128)S(1)} fusion(f32[16,16,32,8]{2,0,3,1:T(8,128)S(1)} %fusion.51, f32[16,32,8,128]{3,0,2,1:T(8,128)S(1)} %convolution_multiply_fusion, s32[16]{0:T(128)S(1)} %iota_add_fusion), kind=kOutput, calls=%fused_computation.80 | convolution fusion | flops 100757504 | bytes 2621504 | tf_op jit(solution)/shard_map/kcxy,yj->jkcx/dot_general | solution.py:37
  366.4 4.4 copy.210
  371.1 15.3 %fusion.81 = f32[32,32]{1,0:T(8,128)S(1)} fusion(bf16[32,8,128,128]{3,2,1,0:T(8,128)(2,1)} %param.5, bf16[32,8,128,128]{3,2,1,0:T(8,128)(2,1)} %copy-done.1), kind=kOutput, calls=%fused_computation.94 | convolution fusion | flops 268435456 | bytes 16781312 | tf_op jit(solution)/shard_map/oxyz,cxyz->oc/dot_general | solution.py:171
  386.4 45.0 %all-reduce = (f32[32,32]{1,0:T(8,128)S(1)}, f32[32]{0:T(128)S(1)}) all-reduce(f32[32,32]{1,0:T(8,128)S(1)} %fusion.81, f32[32]{0:T(128)S(1)} %get-tuple-element.22), channel_id=1, replica_groups=mesh['groups'=2,'mp'=16] {'mp'}, use_global_device_ids=true, to_apply=%region_2.3 | all-reduce | flops 1056 | bytes 8448 | tf_op jit(solution)/shard_map/psum | solution.py:173
  431.4 9.3 %reduce-scatter.5.cloned.1.call-done = f32[16,2,32,16]{2,3,1,0:T(8,128)} async-done(((f32[256,2,32,16]{2,3,1,0:T(8,128)}), f32[16,2,32,16]{2,3,1,0:T(8,128)}) %reduce-scatter.5.cloned.1.call-update) | async-done | bytes 65552 | tf_op jit(solution)/shard_map/reduce_scatter | solution.py:123
  441.7 8.3 %fusion.27 = f32[16,16,1,32]{3,2,1,0:T(1,128)S(1)} fusion(f32[16,32,16,1]{1,3,2,0:T(1,128)S(1)} %bitcast.300, f32[16,2,16,32,32]{4,3,2,1,0:T(8,128)} %param.7), kind=kOutput, calls=%fused_computation.35 | convolution fusion | flops 3145728 | bytes 4259840 | tf_op jit(solution)/shard_map/pok,pkco->pck/dot_general | solution.py:104
  450.0 8.3 %fusion.21 = f32[16,16,1,32]{3,2,1,0:T(1,128)S(1)} fusion(f32[16,32,16,1]{1,3,2,0:T(1,128)S(1)} %bitcast.301, f32[16,2,16,32,32]{4,3,2,1,0:T(8,128)} %param.7), kind=kOutput, calls=%fused_computation.29 | convolution fusion | flops 3145728 | bytes 4259840 | tf_op jit(solution)/shard_map/pok,pkco->pck/dot_general | solution.py:101
  458.4 8.3 %fusion.19 = f32[16,16,1,32]{3,2,1,0:T(1,128)S(1)} fusion(f32[16,32,16,1]{1,3,2,0:T(1,128)S(1)} %bitcast.296, f32[16,2,16,32,32]{4,3,2,1,0:T(8,128)} %param.7), kind=kOutput, calls=%fused_computation.27 | convolution fusion | flops 3145728 | bytes 4259840 | tf_op jit(solution)/shard_map/pok,pkco->pck/dot_general | solution.py:104
  466.7 8.7 %fusion.29 = f32[16,16,1,32]{3,2,1,0:T(1,128)S(1)} fusion(f32[16,32,16,1]{1,3,2,0:T(1,128)S(1)} %bitcast.297, f32[16,2,16,32,32]{4,3,2,1,0:T(8,128)} %param.7), kind=kOutput, calls=%fused_computation.37 | convolution fusion | flops 3145728 | bytes 4259840 | tf_op jit(solution)/shard_map/pok,pkco->pck/dot_general | solution.py:101
  477.4 14.3 %fusion.14 = f32[8,128,128,32]{2,3,1,0:T(8,128)} fusion(bf16[32,8,128,128]{3,2,1,0:T(8,128)(2,1)} %copy-done.1, bf16[32,32]{1,0:T(8,128)(2,1)S(1)} %copy-done), kind=kOutput, calls=%fused_computation.22 | convolution fusion | flops 268435456 | bytes 25167872 | tf_op jit(solution)/shard_map/oc,oxyz->cxyz/dot_general | solution.py:166
  491.8 2.5 add_bitcast_fusion
  494.2 4.5 pad_maximum_fusion
  498.7 31.6 %all-gather.5.cloned.1.call-done = f32[256,2,32,16]{2,3,1,0:T(8,128)} async-done(((f32[16,2,32,16]{2,3,1,0:T(8,128)}), f32[256,2,32,16]{2,3,1,0:T(8,128)}) %all-gather.5.cloned.1.call-update) | async-done | bytes 1048592 | tf_op jit(solution)/shard_map/all_gather | solution.py:129
  530.3 3.9 fusion.328
  534.1 2.7 copy.288
  540.9 2.9 copy.216
  543.8 3.2 fusion.118
  547.0 3.2 fusion.144
  551.2 2.0 copy.220
  553.2 2.0 fusion.142
  557.2 26.8 %fusion.44 = f32[32,8,128,128]{3,2,1,0:T(8,128)S(1)} fusion(f32[16,32,8,128]{3,0,2,1:T(8,128)S(1)} %copy-done.5, f32[16,32,8,128]{3,0,2,1:T(8,128)S(1)} %fusion.120), kind=kOutput, calls=%fused_computation.54 | convolution fusion | flops 805859328 | bytes 20971520 | tf_op jit(solution)/shard_map/kcxy,zk->cxyz/dot_general | solution.py:81
  584.1 32.6 %fusion.10 = bf16[32,8,128,128]{3,2,1,0:T(8,128)(2,1)} fusion(f32[8,128,128,32]{2,3,1,0:T(8,128)} %fusion.14, f32[32,8,128,128]{3,2,1,0:T(8,128)S(1)} %fusion.44, f32[16,32,8,128]{3,0,2,1:T(8,128)S(1)} %fusion.142, f32[16,32,8,128]{3,0,2,1:T(8,128)S(1)} %copy-done.3), kind=kOutput, calls=%fused_computation.15 | convolution fusion | flops 818442240 | bytes 46137344 | tf_op jit(solution)/shard_map/kcxy,zk->cxyz/dot_general | solution.py:81
  (81 shorter events, 33.2 us)
Async XLA Ops:
  7.2 164.0 %copy-start = (bf16[32,32]{1,0:T(8,128)(2,1)S(1)}, bf16[32,32]{1,0:T(8,128)(2,1)}, u32[]{:S(2)}) copy-start(bf16[32,32]{1,0:T(8,128)(2,1)} %param.8) | copy-start | bytes 6148
  7.2 140.4 %reduce-scatter.3.cloned.1.call-start = ((), (), s32[]{:S(2)}) async-start(), calls=%async_computation.2 | async-start | bytes 4456448 | tf_op jit(solution)/shard_map/reduce_scatter | solution.py:123
  7.2 5.8 copy-start.2
  75.7 146.4 %all-gather.3.cloned.1.call-start = ((), (), s32[]{:S(2)}) async-start(), calls=%async_computation.3 | async-start | bytes 4456448 | tf_op jit(solution)/shard_map/all_gather | solution.py:129
  170.7 270.0 %reduce-scatter.5.cloned.1.call-start = ((), (), s32[]{:S(2)}) async-start(), calls=%async_computation.4 | async-start | bytes 4456448 | tf_op jit(solution)/shard_map/reduce_scatter | solution.py:123
  244.9 3.9 copy-start.4
  246.9 30.8 %slice-start = ((s8[8388608]{0:T(1024)(128)(4,1)}), s8[4194304]{0:T(1024)(128)(4,1)S(1)}, s32[]{:S(2)}) async-start(s8[8388608]{0:T(1024)(128)(4,1)} %bitcast.310), calls=%async_computation.6 | async-start | bytes 8388608
  248.8 28.8 %copy-start.6 = (f32[16,32,8,128]{3,0,2,1:T(8,128)S(1)}, f32[16,32,8,128]{3,0,2,1:T(8,128)}, u32[]{:S(2)}) copy-start(f32[16,32,8,128]{3,0,2,1:T(8,128)} %fusion.124) | copy-start | bytes 6291460
  248.9 28.8 %slice-start.1 = ((s8[8388608]{0:T(1024)(128)(4,1)}), s8[4194304]{0:T(1024)(128)(4,1)S(1)}, s32[]{:S(2)}) async-start(s8[8388608]{0:T(1024)(128)(4,1)} %bitcast.310), calls=%async_computation.7 | async-start | bytes 8388608
  248.9 28.8 %copy-start.9 = (f32[32]{0:T(128)S(1)}, f32[32]{0:T(128)}, u32[]{:S(2)}) copy-start(f32[32]{0:T(128)} %param.9) | copy-start | bytes 388
  321.6 20.3 %copy-start.1 = (bf16[32,8,128,128]{3,2,1,0:T(8,128)(2,1)}, bf16[32,8,128,128]{3,2,1,0:T(8,128)(2,1)S(1)}, u32[]{:S(2)}) copy-start(bf16[32,8,128,128]{3,2,1,0:T(8,128)(2,1)S(1)} %get-tuple-element.23) | copy-start | bytes 25165828
  370.9 159.4 %all-gather.5.cloned.1.call-start = ((), (), s32[]{:S(2)}) async-start(), calls=%async_computation.5 | async-start | bytes 4456448 | tf_op jit(solution)/shard_map/all_gather | solution.py:129
  477.4 14.3 %copy-start.7 = (f32[16,16,32]{2,1,0:T(8,128)S(1)}, f32[16,16,32]{2,1,0:T(8,128)}, u32[]{:S(2)}) copy-start(f32[16,16,32]{2,1,0:T(8,128)} %get-tuple-element.12) | copy-start | bytes 98308
  477.4 14.3 %copy-start.8 = (f32[16,16,32]{2,1,0:T(8,128)S(1)}, f32[16,16,32]{2,1,0:T(8,128)}, u32[]{:S(2)}) copy-start(f32[16,16,32]{2,1,0:T(8,128)} %get-tuple-element.13) | copy-start | bytes 98308
  553.2 4.0 copy-start.5
  557.2 26.8 %copy-start.3 = (f32[16,32,8,128]{3,0,2,1:T(8,128)S(1)}, f32[16,32,8,128]{3,0,2,1:T(8,128)}, u32[]{:S(2)}) copy-start(f32[16,32,8,128]{3,0,2,1:T(8,128)} %fusion.118) | copy-start | bytes 6291460
Sparse Core Ops, SparseCore 0:
  75.8 71.7 reduce-scatter.2
  170.8 51.1 all-gather.2
  371.0 69.6 reduce-scatter.4
  476.4 53.8 all-gather.4
where the time goes:
time: 635 us; the launch traced here: 624 us
  matrix products  359 us (57%)
  waiting for transfers between devices  149 us (23%)
  blocking collectives  45 us (7%)
  local copies, waits for them, and re-layouts  44.5 us (7%)
  between operations  14.8 us (2%)
  other arithmetic  9.88 us (2%)
    reduce_scatter x2, waiting for transfers between devices, to_modes(): lax.psum_scatter(spectrum_lines(partial_value, x_cos_mine, x_sin_mine), '...  81.1 us
    dot_general x2, matrix products, space_plane(): jnp.einsum('kcxy,zk->cxyz', b_imag, z_sin, precision=precise)  76.5 us
    all_gather x2, waiting for transfers between devices, to_space(): lax.all_gather(spec, 'mp', axis=0, tiled=True)  68.3 us
    dot_general x2, matrix products, space_plane(): jnp.einsum('kcxy,zk->cxyz', b_real, z_cos, precision=precise)  55.6 us
    psum x1, blocking collectives, shards(): mix_total, bias_total = lax.psum((mix_local, bias_local), 'mp')  45 us
    dot_general x2, matrix products, spectrum_plane(): jnp.einsum('kcxy,yj->jkcx', z_real, y_sin, precision=precise)  29.2 us
    dot_general x2, matrix products, spectrum_plane(): jnp.einsum('kcxy,yj->jkcx', z_real, y_cos, precision=precise)  20.3 us
    dot_general x2, matrix products, spectrum_plane(): jnp.einsum('kcxy,yj->jkcx', z_imag, y_sin, precision=precise)  19.2 us
  transfers between devices with their start and end apart: 4, of which 4 were waited for; matrix products, arithmetic and copies ran while one was open for 8% of the time, Pallas kernels for 0%

commit v1 on v0

v1 whole, which is shorter than its diff:
```python
import functools
import math

import jax
import jax.numpy as jnp
import ml_dtypes
import numpy as np
from jax import lax
from jax.experimental import pallas as pl
from jax.experimental.pallas import tpu as pltpu
from jax.sharding import PartitionSpec as P

C = 32
NX = 128
NY = 128
NZ = 128
KX = 16
KY = 16
KZ = 16
SCALE = 1.0 / (NX * NY * NZ)
OCT = 8
BF = jnp.bfloat16
F32 = jnp.float32
precise = lax.Precision.HIGHEST
VMEM = pl.BlockSpec(memory_space=pltpu.VMEM)


def trig(length, mode_count, signed):
    freqs = np.arange(mode_count) - (mode_count // 2 if signed else 0)
    spots = np.arange(length)
    phases = (spots[:, None] * freqs[None, :] % length) * (2.0 * math.pi / length)
    return np.cos(phases), np.sin(phases)


def low(table):
    return np.asarray(table, np.float32).astype(ml_dtypes.bfloat16)


def tables(rows):
    zc, zs = trig(NZ, KZ, False)
    yc, ys = trig(NY, KY, True)
    xc, xs = trig(NX, KX, True)
    wz = np.where(np.arange(KZ) == 0, 1.0, 2.0) * SCALE
    eye = np.eye(rows)
    fy = np.einsum("syj,xw->sjxwy", np.stack([yc, ys]), eye).reshape(2 * KY * rows, rows * NY)
    gy = np.einsum("syj,xw->xysjw", np.stack([yc, -ys]), eye).reshape(rows * NY, 2 * KY * rows)
    zc_low = low(zc).astype(np.float64)
    zs_low = low(zs).astype(np.float64)
    oct_eye = np.eye(OCT)
    block = np.stack([np.stack([zc_low, -zs_low]), np.stack([-zs_low, -zc_low])])
    fz = np.einsum("srzk,ab->aszrbk", block, oct_eye).reshape(OCT * 2 * NZ, 2 * OCT * KZ)
    fz_w = (fz.reshape(-1, KZ) * wz).reshape(fz.shape)
    back = np.stack([np.stack([zc, zs]), np.stack([-zs, zc])])
    gz = np.einsum("rqzk,ab->rakbqz", back, oct_eye).reshape(2 * OCT * KZ, OCT * 2 * NZ)
    gz_w = (np.einsum("rqzk,ab,k->rakbqz", back, oct_eye, wz)).reshape(gz.shape)
    fx = np.concatenate([xc.T, xs.T], 0).astype(np.float32)
    gx = np.concatenate([xc, xs], 0).astype(np.float32)
    return low(fy), low(gy), low(fz), low(fz_w), low(gz), low(gz_w), fx, gx


def dot(a, b):
    return jnp.dot(a, b, preferred_element_type=F32)


def plane_forward(src, fy, fz, out, rows):
    lines = KY * rows

    @pl.loop(0, C // OCT)
    def _(g):
        parts = []
        for q in range(0, OCT, 2):
            pair = jnp.concatenate([src[g * OCT + q], src[g * OCT + q + 1]], axis=1)
            both = dot(fy[...], pair).astype(BF)
            for h in range(2):
                piece = both[:, h * NZ : (h + 1) * NZ]
                parts += [piece[:lines], piece[lines:]]
        res = dot(jnp.concatenate(parts, axis=1), fz[...])
        half = OCT * KZ
        for r in range(2):
            at = pl.multiple_of(r * C * KZ + g * half, 128)
            out[:, pl.ds(at, half)] = res[:, r * half : (r + 1) * half]


def plane_back(src, gz, gy, out, rows):
    @pl.loop(0, C // OCT)
    def _(g):
        half = OCT * KZ
        lhs = jnp.concatenate(
            [src[:, pl.ds(pl.multiple_of(r * C * KZ + g * half, 128), half)] for r in range(2)],
            axis=1,
        ).astype(BF)
        u = dot(lhs, gz[...]).astype(BF)
        for q in range(0, OCT, 2):
            cols = []
            for h in range(2):
                o = q + h
                cols.append(
                    jnp.concatenate(
                        [u[:, (2 * o + r) * NZ : (2 * o + r + 1) * NZ] for r in range(2)], axis=0
                    )
                )
            res = dot(gy[...], jnp.concatenate(cols, axis=1))
            out[g * OCT + q] = res[:, :NZ]
            out[g * OCT + q + 1] = res[:, NZ:]


def forward_kernel(rows, feat, fy, fz, out):
    plane_forward(feat, fy, fz, out, rows)


TILE = 16


def tile_of(ref, t):
    at = pl.multiple_of(t * TILE, TILE)
    return ref[:, pl.ds(at, TILE), :].reshape(C * TILE, NZ)


def middle_kernel(rows, feat, cot, modes, kron, bias, gz, gy, fy, fz, pg, part, pw, bsum, field, acc, bacc):
    plane_back(modes, gz, gy, field, rows)
    acc[...] = jnp.zeros_like(acc)
    bacc[...] = jnp.zeros_like(bacc)

    @pl.loop(0, rows * NY // (2 * TILE))
    def _(s):
        fs = [tile_of(feat, 2 * s + h) for h in range(2)]
        f = jnp.concatenate(fs, axis=1)
        mix = dot(kron[...], f)
        gs = []
        for h in range(2):
            t = 2 * s + h
            x = mix[:, h * NZ : (h + 1) * NZ] + tile_of(field, t) + bias[...]
            x2 = x * x
            a = math.sqrt(2.0 / math.pi)
            th = jnp.tanh(x * (a + (a * 0.044715) * x2))
            d = 0.5 * (1.0 + th) + (0.5 * x) * (1.0 - th * th) * (a + (3.0 * a * 0.044715) * x2)
            g = (tile_of(cot, t).astype(F32) * d).astype(BF)
            at = pl.multiple_of(t * TILE, TILE)
            pg[:, pl.ds(at, TILE), :] = g.reshape(C, TILE, NZ)
            bacc[...] += g.astype(F32)
            gs.append(g)
        g = jnp.concatenate(gs, axis=1)
        acc[...] += lax.dot_general(g, f, (((1,), (1,)), ((), ())), preferred_element_type=F32)

    n = C * TILE
    ri = lax.broadcasted_iota(jnp.int32, (n, n), 0)
    ci = lax.broadcasted_iota(jnp.int32, (n, n), 1)
    masked = jnp.where(ri % TILE == ci % TILE, acc[...], 0.0)
    rows_sum = jnp.sum(masked.reshape(C, TILE, n), axis=1)
    fold = jnp.where(
        lax.broadcasted_iota(jnp.int32, (n, C), 0) // TILE
        == lax.broadcasted_iota(jnp.int32, (n, C), 1),
        1.0,
        0.0,
    ).astype(F32)
    pw[...] = jnp.dot(rows_sum, fold, precision=precise, preferred_element_type=F32)
    bsum[...] = jnp.sum(bacc[...].reshape(C, TILE, NZ), axis=1)
    plane_forward(pg, fy, fz, part, rows)


def last_kernel(rows, pg, modes, kron, gz, gy, out, field):
    plane_back(modes, gz, gy, field, rows)

    @pl.loop(0, rows * NY // (2 * TILE))
    def _(s):
        f = jnp.concatenate([tile_of(pg, 2 * s + h) for h in range(2)], axis=1)
        mix = dot(kron[...], f)
        for h in range(2):
            t = 2 * s + h
            r = (mix[:, h * NZ : (h + 1) * NZ] + tile_of(field, t)).astype(BF)
            at = pl.multiple_of(t * TILE, TILE)
            out[:, pl.ds(at, TILE), :] = r.reshape(C, TILE, NZ)


def exchange_kernel(n, src, dst, send, recv, own):
    me = lax.axis_index("mp")
    barrier = pltpu.get_barrier_semaphore()

    @pl.loop(1, n)
    def _(s):
        pl.semaphore_signal(
            barrier, inc=1, device_id={"mp": lax.rem(me + s, n)}, device_id_type=pl.DeviceIdType.MESH
        )

    pl.semaphore_wait(barrier, n - 1)

    def copy(peer):
        return pltpu.make_async_remote_copy(
            src_ref=src.at[peer],
            dst_ref=dst.at[me],
            send_sem=send.at[peer],
            recv_sem=recv.at[me],
            device_id={"mp": peer},
            device_id_type=pl.DeviceIdType.MESH,
        )

    def arrival(peer):
        return pltpu.make_async_remote_copy(
            src_ref=src.at[peer],
            dst_ref=dst.at[peer],
            send_sem=send.at[peer],
            recv_sem=recv.at[peer],
            device_id={"mp": peer},
            device_id_type=pl.DeviceIdType.MESH,
        )

    @pl.loop(1, n)
    def _(s):
        copy(lax.rem(me + s, n)).start()

    mine = pltpu.make_async_copy(src.at[me], dst.at[me], own)
    mine.start()
    mine.wait()

    @pl.loop(1, n)
    def _(s):
        peer = lax.rem(me + s, n)
        arrival(peer).wait_recv()
        copy(peer).wait_send()


def exchange(x, n, cid):
    return pl.pallas_call(
        functools.partial(exchange_kernel, n),
        out_shape=jax.ShapeDtypeStruct(x.shape, x.dtype),
        in_specs=[VMEM],
        out_specs=VMEM,
        scratch_shapes=[
            pltpu.SemaphoreType.DMA((n,)),
            pltpu.SemaphoreType.DMA((n,)),
            pltpu.SemaphoreType.DMA,
        ],
        compiler_params=pltpu.CompilerParams(
            collective_id=cid, has_side_effects=True, vmem_limit_bytes=16 << 20
        ),
        name=f"exchange{cid}",
    )(x)


def call(kernel, rows, outs, scratch, args, name):
    return pl.pallas_call(
        functools.partial(kernel, rows),
        out_shape=outs,
        in_specs=[VMEM] * len(args),
        out_specs=jax.tree.map(lambda _: VMEM, outs),
        scratch_shapes=scratch,
        compiler_params=pltpu.CompilerParams(vmem_limit_bytes=60 << 20),
        name=name,
    )(*args)


def to_owner(part, n, rows, cid):
    subs = n // KY
    if subs > 1:
        v = part.reshape(KY, rows, 2 * C, subs, KZ // subs)
        part = jnp.transpose(v, (0, 3, 1, 2, 4))
    blocks = part.reshape(n, rows, 2 * C * KZ // subs)
    return exchange(blocks, n, cid).reshape(NX, 2 * C * KZ // subs)


def to_plane(lines, n, rows, cid):
    subs = n // KY
    got = exchange(lines.reshape(n, rows, lines.shape[1]), n, cid)
    if subs > 1:
        v = got.reshape(KY, subs, rows, 2 * C, KZ // subs)
        got = jnp.transpose(v, (0, 2, 3, 1, 4))
    return got.reshape(KY * rows, 2 * C * KZ)


def lines_forward(g, fx):
    t = jnp.einsum("qx,xl->ql", fx, g, precision=precise).reshape(2, KX, 2, C, -1)
    real = t[0, :, 0] + t[1, :, 1]
    imag = t[0, :, 1] - t[1, :, 0]
    return jnp.transpose(real, (2, 0, 1)), jnp.transpose(imag, (2, 0, 1))


def lines_back(real, imag, gx):
    u = jnp.stack([real, imag])
    u = jnp.transpose(u, (2, 0, 3, 1)).reshape(KX, -1)
    b = jnp.einsum("qa,al->ql", gx, u, precision=precise).reshape(2, NX, 2, -1)
    return jnp.stack([b[0, :, 0] - b[1, :, 1], b[0, :, 1] + b[1, :, 0]], 1).reshape(NX, -1)


def shards(features, cotangent, spectral_weight, pointwise_weight, biases):
    n = lax.axis_size("mp")
    rows = NX // n
    fy, gy, fz, fz_w, gz, gz_w, fx, gx = [jnp.asarray(t) for t in tables(rows)]
    cells = rows * NY
    feat = features.reshape(C, cells, NZ)
    cot = cotangent.reshape(C, cells, NZ)
    eye = jnp.eye(TILE, dtype=BF)
    kron = jnp.kron(pointwise_weight, eye)
    kron_t = jnp.kron(pointwise_weight.T, eye)
    bias = jnp.repeat(biases, TILE)[:, None]
    spread = jax.ShapeDtypeStruct((KY * rows, 2 * C * KZ), F32)
    field = pltpu.VMEM((C, cells, NZ), F32)
    part = call(forward_kernel, rows, spread, [], (feat, fy, fz), "analysis")
    v_r, v_i = lines_forward(to_owner(part, n, rows, 1), fx)
    w_r, w_i = spectral_weight[:, 0], spectral_weight[:, 1]
    s_r, s_i = v_r[..., None], v_i[..., None]
    u_r = jnp.sum(s_r * w_r - s_i * w_i, axis=2)
    u_i = jnp.sum(s_r * w_i + s_i * w_r, axis=2)
    modes = to_plane(lines_back(u_r, u_i, gx), n, rows, 2)
    pg, dpart, pw, bsum = call(
        middle_kernel,
        rows,
        (
            jax.ShapeDtypeStruct((C, cells, NZ), BF),
            spread,
            jax.ShapeDtypeStruct((C, C), F32),
            jax.ShapeDtypeStruct((C, NZ), F32),
        ),
        [field, pltpu.VMEM((C * TILE, C * TILE), F32), pltpu.VMEM((C * TILE, NZ), F32)],
        (feat, cot, modes, kron, bias, gz_w, gy, fy, fz_w),
        "middle",
    )
    d_r, d_i = lines_forward(to_owner(dpart, n, rows, 3), fx)
    e_r, e_i = d_r[:, :, None, :], d_i[:, :, None, :]
    spectral_grad = jnp.stack([s_r * e_r + s_i * e_i, s_r * e_i - s_i * e_r], axis=1)
    m_r = jnp.sum(e_r * w_r + e_i * w_i, axis=3)
    m_i = jnp.sum(e_i * w_r - e_r * w_i, axis=3)
    back = to_plane(lines_back(m_r, m_i, gx), n, rows, 4)
    grad = call(
        last_kernel,
        rows,
        jax.ShapeDtypeStruct((C, cells, NZ), BF),
        [field],
        (pg, back, kron_t, gz, gy),
        "synthesis",
    )
    factor = float(NX * NY * NZ) ** (-0.5)
    sums = jnp.concatenate([pw, jnp.sum(bsum, axis=1)[:, None]], axis=1)
    total = jnp.sum(lax.all_gather(sums, "mp"), axis=0) * factor
    return (grad.reshape(features.shape), spectral_grad, total[:, :C], total[:, C])


def solution(mesh):
    return jax.shard_map(
        shards,
        mesh=mesh,
        in_specs=(
            P(None, ("groups", "mp"), None, None),
            P(None, ("groups", "mp"), None, None),
            P("mp", None, None, None, None),
            P(),
            P(),
        ),
        out_specs=(
            P(None, ("groups", "mp"), None, None),
            P(("groups", "mp"), None, None, None, None),
            P("groups", None),
            P("groups"),
        ),
        check_vma=False,
    )
```

time: 635 us -> 221 us (0.35); the launches traced: 624 us -> 221 us
  matrix products: 359 us -> 2.71 us
  Pallas kernels: 0 us -> 149 us
  waiting for transfers between devices: 149 us -> 0 us
  blocking collectives: 45 us -> 15.3 us
  local copies, waits for them, and re-layouts: 44.5 us -> 28.6 us
  other arithmetic: 9.88 us -> 24.6 us
  between operations: 14.8 us -> 0.93 us
    dot_general x51 -> x4, matrix products: 359 us -> 2.71 us  [the longest x2 1.92 us: lines_back(): b = jnp.einsum('qa,al->ql', gx, u, precision=precise).reshape(2, NX, 2, -1)]
    pallas_call x0 -> x7, Pallas kernels: none -> 149 us  [the longest x3 78.6 us: call(): pl.pallas_call(functools.partial(kernel, rows), out_shape=outs, in_specs=...]
    reduce_scatter x2 -> x0, waiting for transfers between devices: 81.1 us -> none  [to_modes(): lax.psum_scatter(spectrum_lines(partial_value, x_cos_mine, x_sin_mine), '...]
    all_gather x2 -> x0, waiting for transfers between devices: 68.3 us -> none  [to_space(): lax.all_gather(spec, 'mp', axis=0, tiled=True)]
    psum x1 -> x0, blocking collectives: 45 us -> none  [shards(): mix_total, bias_total = lax.psum((mix_local, bias_local), 'mp')]
    mul x0 -> x2, local copies, waits for them, and re-layouts: none -> 16.8 us  [the longest x1 8.4 us: shards(): kron = jnp.kron(pointwise_weight, eye)]
    all_gather x0 -> x1, blocking collectives: none -> 15.3 us  [shards(): total = jnp.sum(lax.all_gather(sums, 'mp'), axis=0) * factor]
    squeeze x10 -> x0, local copies, waits for them, and re-layouts: 13.9 us -> none  [the longest x2 5.85 us: space_plane(): q_real = grid[:, :, 0]]
  transfers between devices with their start and end apart: 4 -> 0, of which waited for: 4 -> 0; matrix products, arithmetic and copies ran while one was open for 8% -> 0% of each run, Pallas kernels for 0% -> 0%
where the time goes in v1:
time: 221 us
  Pallas kernels  149 us (67%)
  local copies, waits for them, and re-layouts  28.6 us (13%)
  other arithmetic  24.6 us (11%)
  blocking collectives  15.3 us (7%)
  matrix products  2.71 us (1%)
    pallas_call x3, Pallas kernels, call(): pl.pallas_call(functools.partial(kernel, rows), out_shape=outs, in_specs=...  78.6 us
    pallas_call x4, Pallas kernels, exchange(): pl.pallas_call(functools.partial(exchange_kernel, n), out_shape=jax.Shape...  70 us
    all_gather x1, blocking collectives, shards(): total = jnp.sum(lax.all_gather(sums, 'mp'), axis=0) * factor  15.3 us
    mul x1, local copies, waits for them, and re-layouts, shards(): kron = jnp.kron(pointwise_weight, eye)  8.4 us
    mul x1, local copies, waits for them, and re-layouts, shards(): kron_t = jnp.kron(pointwise_weight.T, eye)  8.4 us
    reduce_sum x1, other arithmetic, shards(): u_r = jnp.sum(s_r * w_r - s_i * w_i, axis=2)  5.54 us
    reduce_sum x1, other arithmetic, shards(): m_r = jnp.sum(e_r * w_r + e_i * w_i, axis=3)  4.66 us
    another operation x1, other arithmetic, shards(): jnp.stack([s_r * e_r + s_i * e_i, s_r * e_i - s_i * e_r], axis=1)  4.47 us

profile of v1, /device:TPU:15, one launch (start us, length us, event | category | flops | bytes accessed | tf_op | source)
XLA Modules:
  0.0 220.8 jit_solution(10251090841884720787)
XLA Ops:
  0.6 0.8 copy.48
  1.4 0.7 broadcast_in_dim.16
  2.2 0.9 broadcast_in_dim_reshape.4.bias
  3.0 8.6 %analysis.1 = f32[128,1024]{1,0:T(8,128)} custom-call(bf16[32,1024,128]{2,1,0:T(8,128)(2,1)} %bitcast.103, bf16[256,1024]{1,0:T(8,128)(2,1)} %constant.20.clone.fy, bf16[2048,256]{1,0:T(8,128)(2,1)} %constant.22.clone.fz), custom_call_target="tpu_custom_call" | custom-call | tf_op jit(solution)/shard_map/analysis/pallas_call | solution.py:241
  11.6 1.0 copy-done.1
  12.7 16.7 %exchange1.1 = f32[16,8,1024]{2,1,0:T(8,128)S(1)} custom-call(f32[16,8,1024]{2,1,0:T(8,128)S(1)} %bitcast.100), custom_call_target="tpu_custom_call" | custom-call | tf_op jit(solution)/shard_map/exchange1/pallas_call | solution.py:223
  29.4 0.4 fusion.10
  29.8 0.4 reshape.198
  30.3 0.1 copy.40
  30.4 0.1 copy.42
  30.6 5.5 %fusion.1 = (f32[16,16,32]{2,1,0:T(8,128)S(1)}, f32[16,16,32]{2,1,0:T(8,128)S(1)}) fusion(f32[16,2,16,32,32]{4,3,2,1,0:T(8,128)} %param.15, f32[16,16,32]{2,1,0:T(8,128)S(1)} %copy.42, f32[16,16,32]{2,1,0:T(8,128)S(1)} %copy.40), kind=kLoop, calls=%fused_computation.6 | loop fusion | flops 2080768 | bytes 2228224 | tf_op jit(solution)/shard_map/reduce_sum | solution.py:301
  36.2 0.2 copy.43
  36.4 0.3 reshape.199
  36.7 1.0 fusion.21
  37.6 0.9 reshape.200
  38.5 0.5 fusion.17
  39.1 0.5 pad_maximum_fusion.1
  39.6 0.5 reshape_reshape.6.src
  40.0 16.3 %exchange2.1 = f32[16,8,1024]{2,1,0:T(8,128)S(1)} custom-call(f32[16,8,1024]{2,1,0:T(8,128)S(1)} %reshape_reshape.6.src), custom_call_target="tpu_custom_call" | custom-call | tf_op jit(solution)/shard_map/exchange2/pallas_call | solution.py:223
  56.3 0.8 copy-done.2
  57.1 3.7 %broadcast_multiply_fusion = (bf16[32,16,32,16]{3,2,1,0:T(8,128)(2,1)}, bf16[32,16,32,16]{3,2,1,0:T(8,128)(2,1)}) fusion(bf16[32,32]{1,0:T(8,128)(2,1)S(1)} %copy.48, bf16[16,16]{1,0:T(8,128)(2,1)S(1)} %fusion.20, bf16[32,32]{1,0:T(8,128)(2,1)S(1)} %copy-done.7), kind=kLoop, calls=%fused_computation.19 | loop fusion | flops 524288 | bytes 1053184 | tf_op jit(solution)/shard_map/jit(kron)/mul | solution.py:293
  60.8 8.4 %mul.193.kron = bf16[512,512]{1,0:T(8,128)(2,1)} reshape(bf16[32,16,32,16]{3,2,1,0:T(8,128)(2,1)} %get-tuple-element.26) | data formatting | bytes 1048576 | tf_op jit(solution)/shard_map/jit(kron)/mul | solution.py:293
  69.2 8.4 %mul.184.kron = bf16[512,512]{1,0:T(8,128)(2,1)} reshape(bf16[32,16,32,16]{3,2,1,0:T(8,128)(2,1)} %get-tuple-element.27) | data formatting | bytes 1048576 | tf_op jit(solution)/shard_map/jit(kron)/mul | solution.py:292
  77.6 48.5 %middle.1 = (bf16[32,1024,128]{2,1,0:T(8,128)(2,1)}, f32[128,1024]{1,0:T(8,128)}, f32[32,32]{1,0:T(8,128)}, f32[32,128]{1,0:T(8,128)}) custom-call(bf16[32,1024,128]{2,1,0:T(8,128)(2,1)} %bitcast.104, bf16[32,1024,128]{2,1,0:T(8,128)(2,1)} %bitcast.106, f32[128,1024]{1,0:T(8,128)} %bitcast.101, bf16[512,512]{1,0:T(8,128)(2,1)} %mul.184.kron, ...), custom_call_target="tpu_custom_call" | custom-call | tf_op jit(solution)/shard_map/middle/pallas_call | solution.py:241
  126.1 1.0 copy-done.3
  127.2 16.0 %exchange3.1 = f32[16,8,1024]{2,1,0:T(8,128)S(1)} custom-call(f32[16,8,1024]{2,1,0:T(8,128)S(1)} %bitcast.102), custom_call_target="tpu_custom_call" | custom-call | tf_op jit(solution)/shard_map/exchange3/pallas_call | solution.py:223
  143.2 0.4 fusion.8
  143.6 0.8 reduce_sum.58
  144.4 0.1 copy.53
  144.5 0.8 pad_maximum_fusion.3
  145.3 15.3 %all-gather = f32[512,33]{1,0:T(8,128)S(1)} all-gather(f32[32,33]{1,0:T(8,128)S(1)} %pad_maximum_fusion.3), channel_id=2, replica_groups=mesh['groups'=2,'mp'=16] {'mp'}, dimensions={0}, use_global_device_ids=true | all-gather | bytes 71808 | tf_op jit(solution)/shard_map/all_gather | solution.py:333
  160.7 0.7 slice_reduce_fusion
  161.4 0.4 reshape.204
  161.8 0.1 copy.45
  162.0 0.1 copy.46
  162.1 4.7 %fusion.5 = (f32[16,16,32]{2,1,0:T(8,128)S(1)}, f32[16,16,32]{2,1,0:T(8,128)S(1)}) fusion(f32[16,2,16,32,32]{4,3,2,1,0:T(8,128)} %param.15, f32[16,16,32]{2,1,0:T(8,128)S(1)} %copy.46, f32[16,16,32]{2,1,0:T(8,128)S(1)} %copy.45), kind=kLoop, calls=%fused_computation.10 | loop fusion | flops 2080768 | bytes 2228224 | tf_op jit(solution)/shard_map/reduce_sum | solution.py:320
  166.8 0.2 copy.47
  167.0 0.3 reshape.205
  167.3 1.0 fusion.22
  168.3 0.9 reshape.206
  169.2 0.5 fusion.13
  169.7 0.5 pad_maximum_fusion.2
  170.2 0.5 reshape_reshape.7.src
  170.7 21.0 %exchange4.1 = f32[16,8,1024]{2,1,0:T(8,128)S(1)} custom-call(f32[16,8,1024]{2,1,0:T(8,128)S(1)} %reshape_reshape.7.src), custom_call_target="tpu_custom_call" | custom-call | tf_op jit(solution)/shard_map/exchange4/pallas_call | solution.py:223
  191.7 0.8 copy-done
  192.5 21.5 %synthesis.1 = bf16[32,1024,128]{2,1,0:T(8,128)(2,1)} custom-call(bf16[32,1024,128]{2,1,0:T(8,128)(2,1)} %get-tuple-element.8.pg, f32[128,1024]{1,0:T(8,128)} %bitcast.99, bf16[512,512]{1,0:T(8,128)(2,1)} %mul.193.kron, bf16[256,2048]{1,0:T(8,128)(2,1)} %constant.24.clone.gz, bf16[1024,256]{1,0:T(8,128)(2,1)} %constant.21.clone.gy), custom_call_target="tpu_custom_call" | custom-call | tf_op jit(solution)/shard_map/synthesis/pallas_call | solution.py:241
  214.0 2.3 %multiply_add_fusion = (f32[16,1,16,32,32]{4,3,2,1,0:T(8,128)S(1)}, f32[16,1,16,32,32]{4,3,2,1,0:T(8,128)S(1)}) fusion(f32[16,16,32]{2,1,0:T(8,128)S(1)} %copy.46, f32[16,16,32]{2,1,0:T(8,128)S(1)} %copy.42, f32[16,16,32]{2,1,0:T(8,128)S(1)} %copy.45, f32[16,16,32]{2,1,0:T(8,128)S(1)} %copy.40), kind=kLoop, calls=%fused_computation.18 | loop fusion | flops 1572864 | bytes 2228224 | tf_op jit(solution)/shard_map/add | solution.py:319
  216.3 4.5 %pad_maximum_fusion = f32[16,2,16,32,32]{4,3,2,1,0:T(8,128)} fusion(f32[16,1,16,32,32]{4,3,2,1,0:T(8,128)S(1)} %get-tuple-element.25, f32[16,1,16,32,32]{4,3,2,1,0:T(8,128)S(1)} %get-tuple-element.24), kind=kLoop, calls=%fused_computation | loop fusion | flops 524288 | bytes 4194304 | tf_op jit(solution)/shard_map/stack | solution.py:319
  (19 shorter events, 0.3 us)
Async XLA Ops:
  3.0 26.4 %copy-start.6 = (f32[32,128]{1,0:T(8,128)S(1)}, f32[32,128]{1,0:T(8,128)}, u32[]{:S(2)}) copy-start(f32[32,128]{1,0:T(8,128)} %constant.26.clone) | copy-start | bytes 49156
  11.6 1.0 copy-start.1
  30.6 6.1 %copy-start.4 = (f32[256,16]{1,0:T(8,128)S(1)}, f32[256,16]{1,0:T(8,128)}, u32[]{:S(2)}) copy-start(f32[256,16]{1,0:T(8,128)} %constant.27.clone) | copy-start | bytes 49156
  36.4 20.7 %copy-start.7 = (bf16[32,32]{1,0:T(8,128)(2,1)S(1)}, bf16[32,32]{1,0:T(8,128)(2,1)}, u32[]{:S(2)}) copy-start(bf16[32,32]{1,0:T(8,128)(2,1)} %param.16) | copy-start | bytes 6148
  56.3 0.8 copy-start.2
  126.1 1.0 copy-start.3
  160.7 6.1 %copy-start.5 = (f32[32,33]{1,0:T(8,128)}, f32[32,33]{1,0:T(8,128)S(1)}, u32[]{:S(2)}) copy-start(f32[32,33]{1,0:T(8,128)S(1)} %broadcast_multiply_fusion.2) | copy-start | bytes 12676
  191.7 0.8 copy-start

commit v2 on v1

v2 whole, which is shorter than its diff:
```python
import functools
import math

import jax
import jax.numpy as jnp
import ml_dtypes
import numpy as np
from jax import lax
from jax.experimental import pallas as pl
from jax.experimental.pallas import tpu as pltpu
from jax.sharding import PartitionSpec as P

C = 32
NX = 128
NY = 128
NZ = 128
KX = 16
KY = 16
KZ = 16
SCALE = 1.0 / (NX * NY * NZ)
OCT = 8
GROUPS = C // OCT
GLANES = 2 * OCT * KZ
LANES = 128
SAVES = 4
BF = jnp.bfloat16
F32 = jnp.float32
precise = lax.Precision.HIGHEST
VMEM = pl.BlockSpec(memory_space=pltpu.VMEM)
HBM = pl.BlockSpec(memory_space=pl.ANY)


def trig(length, mode_count, signed):
    freqs = np.arange(mode_count) - (mode_count // 2 if signed else 0)
    spots = np.arange(length)
    phases = (spots[:, None] * freqs[None, :] % length) * (2.0 * math.pi / length)
    return np.cos(phases), np.sin(phases)


def low(table):
    return np.asarray(table, np.float32).astype(ml_dtypes.bfloat16)


def tables(rows):
    zc, zs = trig(NZ, KZ, False)
    yc, ys = trig(NY, KY, True)
    xc, xs = trig(NX, KX, True)
    wz = np.where(np.arange(KZ) == 0, 1.0, 2.0) * SCALE
    eye = np.eye(rows)
    fy = np.einsum("syj,xw->sjxwy", np.stack([yc, ys]), eye).reshape(2 * KY * rows, rows * NY)
    gy = np.einsum("syj,xw->xysjw", np.stack([yc, -ys]), eye).reshape(rows * NY, 2 * KY * rows)
    zc_low = low(zc).astype(np.float64)
    zs_low = low(zs).astype(np.float64)
    oct_eye = np.eye(OCT)
    block = np.stack([np.stack([zc_low, -zs_low]), np.stack([-zs_low, -zc_low])])
    fz = np.einsum("srzk,ab->aszrbk", block, oct_eye).reshape(OCT * 2 * NZ, 2 * OCT * KZ)
    fz_w = (fz.reshape(-1, KZ) * wz).reshape(fz.shape)
    back = np.stack([np.stack([zc, zs]), np.stack([-zs, zc])])
    gz = np.einsum("rqzk,ab->rakbqz", back, oct_eye).reshape(2 * OCT * KZ, OCT * 2 * NZ)
    gz_w = (np.einsum("rqzk,ab,k->rakbqz", back, oct_eye, wz)).reshape(gz.shape)
    fx = np.concatenate([xc.T, xs.T], 0).astype(np.float32)
    gx = np.concatenate([xc, xs], 0).astype(np.float32)
    return low(fy), low(gy), low(fz), low(fz_w), low(gz), low(gz_w), fx, gx


def dot(a, b):
    return jnp.dot(a, b, preferred_element_type=F32)


def forward_group(src, g, fy, fz, lines):
    parts = []
    for q in range(0, OCT, 2):
        pair = jnp.concatenate([src[g * OCT + q], src[g * OCT + q + 1]], axis=1)
        both = dot(fy[...], pair).astype(BF)
        for h in range(2):
            piece = both[:, h * NZ : (h + 1) * NZ]
            parts += [piece[:lines], piece[lines:]]
    return dot(jnp.concatenate(parts, axis=1), fz[...])


def plane_back(src, gz, gy, out):
    @pl.loop(0, GROUPS)
    def _(g):
        lhs = src[:, pl.ds(pl.multiple_of(g * GLANES, GLANES), GLANES)].astype(BF)
        u = dot(lhs, gz[...]).astype(BF)
        for q in range(0, OCT, 2):
            cols = []
            for h in range(2):
                o = q + h
                cols.append(
                    jnp.concatenate(
                        [u[:, (2 * o + r) * NZ : (2 * o + r + 1) * NZ] for r in range(2)], axis=0
                    )
                )
            res = dot(gy[...], jnp.concatenate(cols, axis=1))
            out[g * OCT + q] = res[:, :NZ]
            out[g * OCT + q + 1] = res[:, NZ:]


def plain_forward(src, fy, fz, out, lines):
    @pl.loop(0, GROUPS)
    def _(g):
        at = pl.multiple_of(g * GLANES, GLANES)
        out[:, pl.ds(at, GLANES)] = forward_group(src, g, fy, fz, lines)


def load_groups(hbm, buf, sems):
    copies = []
    for g in range(GROUPS):
        part = pl.ds(g * OCT, OCT)
        copies.append(pltpu.make_async_copy(hbm.at[part], buf.at[part], sems.at[g]))
        copies[-1].start()
    return copies


def greet(n):
    me = lax.axis_index("mp")

    @pl.loop(1, n)
    def _(s):
        pl.semaphore_signal(
            pltpu.get_barrier_semaphore(),
            inc=1,
            device_id={"mp": lax.rem(me + s, n)},
            device_id_type=pl.DeviceIdType.MESH,
        )


def remote(src, dst, send, recv, peer):
    return pltpu.make_async_remote_copy(
        src_ref=src,
        dst_ref=dst,
        send_sem=send,
        recv_sem=recv,
        device_id={"mp": peer},
        device_id_type=pl.DeviceIdType.MESH,
    )


def analysis_kernel(rows, n, feat_hbm, fy, fz, dst, feat, src, load, send, recv, own):
    me = lax.axis_index("mp")
    greet(n)
    loads = load_groups(feat_hbm, feat, load)
    mine = []
    wide = GLANES * GROUPS // 2
    for half in range(2):
        for g in range(half * GROUPS // 2, (half + 1) * GROUPS // 2):
            loads[g].wait()
            res = forward_group(feat, g, fy, fz, KY * rows)
            src[:, :, g * GLANES : (g + 1) * GLANES] = res.reshape(KY, rows, GLANES)
        lanes = pl.ds(half * wide, wide)
        if half == 0:
            pl.semaphore_wait(pltpu.get_barrier_semaphore(), n - 1)

        @pl.loop(1, n)
        def _(s):
            peer = lax.rem(me + s, n)
            remote(
                src.at[peer, :, lanes],
                dst.at[me, :, lanes],
                send.at[half, peer],
                recv.at[half, me],
                peer,
            ).start()

        mine.append(pltpu.make_async_copy(src.at[me, :, lanes], dst.at[me, :, lanes], own.at[half]))
        mine[-1].start()
    for half in range(2):
        lanes = pl.ds(half * wide, wide)
        mine[half].wait()

        @pl.loop(1, n)
        def _(s):
            peer = lax.rem(me + s, n)
            both = remote(
                src.at[peer, :, lanes],
                dst.at[peer, :, lanes],
                send.at[half, peer],
                recv.at[half, peer],
                peer,
            )
            both.wait_recv()
            both.wait_send()


def forward_kernel(rows, feat, fy, fz, out):
    plain_forward(feat, fy, fz, out, KY * rows)


TILE = 16
STEP = 4


def tile_of(ref, t):
    at = pl.multiple_of(t * TILE, TILE)
    return ref[:, pl.ds(at, TILE), :].reshape(C * TILE, NZ)


def put_tile(ref, t, value):
    at = pl.multiple_of(t * TILE, TILE)
    ref[:, pl.ds(at, TILE), :] = value.reshape(C, TILE, NZ)


def widen(weight):
    n = C * TILE
    row = lax.broadcasted_iota(jnp.int32, (n, C), 0) // TILE
    up = jnp.where(row == lax.broadcasted_iota(jnp.int32, (n, C), 1), 1.0, 0.0).astype(BF)
    left = dot(up, weight).astype(BF)
    full = lax.dot_general(left, up, (((1,), (1,)), ((), ())), preferred_element_type=F32)
    ri = lax.broadcasted_iota(jnp.int32, (n, n), 0)
    ci = lax.broadcasted_iota(jnp.int32, (n, n), 1)
    return jnp.where(ri % TILE == ci % TILE, full, 0.0).astype(BF)


def middle_kernel(
    rows, feat_hbm, cot_hbm, modes, weight, bias, gz, gy, fy, fz, pg_hbm, part, sums,
    field, acc, bacc, kron, feat, cot, pg, fsem, csem, psem,
):
    loads = load_groups(feat_hbm, feat, fsem) + load_groups(cot_hbm, cot, csem)
    kron[...] = widen(weight[...])
    acc[...] = jnp.zeros_like(acc)
    bacc[...] = jnp.zeros_like(bacc)
    plane_back(modes, gz, gy, field)
    for copy in loads:
        copy.wait()

    @pl.loop(0, rows * NY // (STEP * TILE))
    def _(s):
        f = jnp.concatenate([tile_of(feat, STEP * s + h) for h in range(STEP)], axis=1)
        mix = dot(kron[...], f)
        gs = []
        for h in range(STEP):
            t = STEP * s + h
            x = mix[:, h * NZ : (h + 1) * NZ] + tile_of(field, t) + bias[...]
            x2 = x * x
            a = math.sqrt(2.0 / math.pi)
            th = jnp.tanh(x * (a + (a * 0.044715) * x2))
            d = (0.5 + 0.5 * th) * (1.0 + (x * (1.0 - th)) * (a + (3.0 * a * 0.044715) * x2))
            g = (tile_of(cot, t).astype(F32) * d).astype(BF)
            put_tile(pg, t, g)
            gs.append(g)
        bacc[...] += sum(g.astype(F32) for g in gs)
        g = jnp.concatenate(gs, axis=1)
        acc[...] += lax.dot_general(g, f, (((1,), (1,)), ((), ())), preferred_element_type=F32)

    save = pltpu.make_async_copy(pg, pg_hbm, psem)
    save.start()
    n = C * TILE
    ri = lax.broadcasted_iota(jnp.int32, (n, n), 0)
    ci = lax.broadcasted_iota(jnp.int32, (n, n), 1)
    masked = jnp.where(ri % TILE == ci % TILE, acc[...], 0.0)
    rows_sum = jnp.sum(masked.reshape(C, TILE, n), axis=1)
    fold = jnp.where(
        lax.broadcasted_iota(jnp.int32, (n, LANES), 0) // TILE
        == lax.broadcasted_iota(jnp.int32, (n, LANES), 1),
        1.0,
        0.0,
    ).astype(F32)
    pw = jnp.dot(rows_sum, fold, precision=precise, preferred_element_type=F32)
    by_row = jnp.sum(bacc[...].reshape(C, TILE, NZ), axis=1)
    lane = lax.broadcasted_iota(jnp.int32, (C, LANES), 1)
    sums[...] = pw + jnp.where(lane == C, jnp.sum(by_row, axis=1, keepdims=True), 0.0)
    plain_forward(pg, fy, fz, part, KY * rows)
    save.wait()


def last_kernel(rows, pg_hbm, modes, weight, gz, gy, out_hbm, field, kron, pg, out, fsem, osem):
    loads = load_groups(pg_hbm, pg, fsem)
    kron[...] = widen(weight[...])
    plane_back(modes, gz, gy, field)
    for copy in loads:
        copy.wait()
    saves = []
    cells = rows * NY // SAVES
    for piece in range(SAVES):

        @pl.loop(0, cells // (STEP * TILE))
        def _(i):
            s = piece * (cells // (STEP * TILE)) + i
            f = jnp.concatenate([tile_of(pg, STEP * s + h) for h in range(STEP)], axis=1)
            mix = dot(kron[...], f)
            for h in range(STEP):
                t = STEP * s + h
                r = mix[:, h * NZ : (h + 1) * NZ] + tile_of(field, t)
                put_tile(out, t, r.astype(BF))

        at = pl.ds(piece * cells, cells)
        saves.append(pltpu.make_async_copy(out.at[:, at], out_hbm.at[:, at], osem.at[piece]))
        saves[-1].start()
    for copy in saves:
        copy.wait()


def exchange_kernel(n, arrays, *refs):
    srcs, dsts = refs[:arrays], refs[arrays : 2 * arrays]
    send, recv, own = refs[2 * arrays :]
    me = lax.axis_index("mp")
    greet(n)
    pl.semaphore_wait(pltpu.get_barrier_semaphore(), n - 1)

    @pl.loop(1, n)
    def _(s):
        peer = lax.rem(me + s, n)
        for i in range(arrays):
            remote(
                srcs[i].at[peer], dsts[i].at[me], send.at[i, peer], recv.at[i, me], peer
            ).start()

    for i in range(arrays):
        mine = pltpu.make_async_copy(srcs[i].at[me], dsts[i].at[me], own.at[i])
        mine.start()
        mine.wait()

    @pl.loop(1, n)
    def _(s):
        peer = lax.rem(me + s, n)
        for i in range(arrays):
            both = remote(
                srcs[i].at[peer], dsts[i].at[peer], send.at[i, peer], recv.at[i, peer], peer
            )
            both.wait_recv()
            both.wait_send()


def exchange(xs, n, cid):
    return pl.pallas_call(
        functools.partial(exchange_kernel, n, len(xs)),
        out_shape=[jax.ShapeDtypeStruct(x.shape, x.dtype) for x in xs],
        in_specs=[VMEM] * len(xs),
        out_specs=[VMEM] * len(xs),
        scratch_shapes=[
            pltpu.SemaphoreType.DMA((len(xs), n)),
            pltpu.SemaphoreType.DMA((len(xs), n)),
            pltpu.SemaphoreType.DMA((len(xs),)),
        ],
        compiler_params=pltpu.CompilerParams(
            collective_id=cid, has_side_effects=True, vmem_limit_bytes=16 << 20
        ),
        name=f"exchange{cid}",
    )(*xs)


def call(kernel, rows, outs, scratch, args, name, far=(), far_out=(), cid=None):
    outs = list(outs)
    params = {} if cid is None else {"collective_id": cid, "has_side_effects": True}
    return pl.pallas_call(
        functools.partial(kernel, rows),
        out_shape=outs,
        in_specs=[HBM if i in far else VMEM for i in range(len(args))],
        out_specs=[HBM if i in far_out else VMEM for i in range(len(outs))],
        scratch_shapes=scratch,
        compiler_params=pltpu.CompilerParams(vmem_limit_bytes=60 << 20, **params),
        name=name,
    )(*args)


def owner_blocks(part, n, rows):
    subs = n // KY
    if subs > 1:
        v = part.reshape(KY, rows, 2 * C, subs, KZ // subs)
        part = jnp.transpose(v, (0, 3, 1, 2, 4))
    return part.reshape(n, rows, 2 * C * KZ // subs)


def plane_blocks(got, n, rows):
    subs = n // KY
    if subs > 1:
        v = got.reshape(KY, subs, rows, 2 * C, KZ // subs)
        got = jnp.transpose(v, (0, 2, 3, 1, 4))
    return got.reshape(KY * rows, 2 * C * KZ)


def lines_forward(g, fx):
    g = g.reshape(NX, -1)
    t = jnp.einsum("qx,xl->ql", fx, g, precision=precise).reshape(2, KX, GROUPS, 2, OCT, -1)
    real = t[0, :, :, 0] + t[1, :, :, 1]
    imag = t[0, :, :, 1] - t[1, :, :, 0]
    real, imag = (jnp.transpose(v.reshape(KX, C, -1), (2, 0, 1)) for v in (real, imag))
    return real, imag


def lines_back(real, imag, gx, n, rows):
    u = jnp.stack([real, imag]).reshape(2, real.shape[0], KX, GROUPS, OCT)
    u = jnp.transpose(u, (2, 3, 0, 4, 1)).reshape(KX, -1)
    b = jnp.einsum("qa,al->ql", gx, u, precision=precise).reshape(2, NX, GROUPS, 2, -1)
    lines = jnp.stack([b[0, :, :, 0] - b[1, :, :, 1], b[0, :, :, 1] + b[1, :, :, 0]], 2)
    return lines.reshape(n, rows, -1)


def shards(features, cotangent, spectral_weight, pointwise_weight, biases):
    n = lax.axis_size("mp")
    rows = NX // n
    fy, gy, fz, fz_w, gz, gz_w, fx, gx = [jnp.asarray(t) for t in tables(rows)]
    cells = rows * NY
    feat = features.reshape(C, cells, NZ)
    cot = cotangent.reshape(C, cells, NZ)
    bias = jnp.repeat(biases, TILE)[:, None]
    spread = jax.ShapeDtypeStruct((KY * rows, 2 * C * KZ), F32)
    whole = jax.ShapeDtypeStruct((C, cells, NZ), BF)
    field = pltpu.VMEM((C, cells, NZ), F32)
    block = pltpu.VMEM((C, cells, NZ), BF)
    wide = C * TILE
    sems = pltpu.SemaphoreType.DMA((GROUPS,))
    if n == KY:
        blocks = jax.ShapeDtypeStruct((n, rows, 2 * C * KZ), F32)
        dma = pltpu.SemaphoreType.DMA
        got = call(
            lambda r, *refs: analysis_kernel(r, n, *refs),
            rows,
            [blocks],
            [block, pltpu.VMEM(blocks.shape, F32), sems, dma((2, n)), dma((2, n)), dma((2,))],
            (feat, fy, fz),
            "analysis",
            far=(0,),
            cid=1,
        )[0]
    else:
        part = call(forward_kernel, rows, [spread], [], (feat, fy, fz), "analysis")[0]
        got = exchange([owner_blocks(part, n, rows)], n, 1)[0]
    v_r, v_i = lines_forward(got, fx)
    w_r, w_i = spectral_weight[:, 0], spectral_weight[:, 1]
    s_r, s_i = v_r[..., None], v_i[..., None]
    u_r = jnp.sum(s_r * w_r - s_i * w_i, axis=2)
    u_i = jnp.sum(s_r * w_i + s_i * w_r, axis=2)
    modes = plane_blocks(exchange([lines_back(u_r, u_i, gx, n, rows)], n, 2)[0], n, rows)
    pg, dpart, sums = call(
        middle_kernel,
        rows,
        [whole, spread, jax.ShapeDtypeStruct((C, LANES), F32)],
        [
            field,
            pltpu.VMEM((wide, wide), F32),
            pltpu.VMEM((wide, NZ), F32),
            pltpu.VMEM((wide, wide), BF),
            block,
            block,
            block,
            sems,
            sems,
            pltpu.SemaphoreType.DMA,
        ],
        (feat, cot, modes, pointwise_weight, bias, gz_w, gy, fy, fz_w),
        "middle",
        far=(0, 1),
        far_out=(0,),
    )
    got, got_sums = exchange(
        [owner_blocks(dpart, n, rows), sums.reshape(n, C // n, LANES)], n, 3
    )
    d_r, d_i = lines_forward(got, fx)
    e_r, e_i = d_r[:, :, None, :], d_i[:, :, None, :]
    m_r = jnp.sum(e_r * w_r + e_i * w_i, axis=3)
    m_i = jnp.sum(e_i * w_r - e_r * w_i, axis=3)
    mine = jnp.broadcast_to(jnp.sum(got_sums, axis=0), (n, C // n, LANES))
    back, total = exchange([lines_back(m_r, m_i, gx, n, rows), mine], n, 4)
    spectral_grad = jnp.stack([s_r * e_r + s_i * e_i, s_r * e_i - s_i * e_r], axis=1)
    grad = call(
        last_kernel,
        rows,
        [whole],
        [field, pltpu.VMEM((wide, wide), BF), block, block, sems, pltpu.SemaphoreType.DMA((SAVES,))],
        (pg, plane_blocks(back, n, rows), pointwise_weight.T, gz, gy),
        "synthesis",
        far=(0,),
        far_out=(0,),
    )[0]
    factor = float(NX * NY * NZ) ** (-0.5)
    total = total.reshape(C, LANES) * factor
    return (grad.reshape(features.shape), spectral_grad, total[:, :C], total[:, C])


def solution(mesh):
    return jax.shard_map(
        shards,
        mesh=mesh,
        in_specs=(
            P(None, ("groups", "mp"), None, None),
            P(None, ("groups", "mp"), None, None),
            P("mp", None, None, None, None),
            P(),
            P(),
        ),
        out_specs=(
            P(None, ("groups", "mp"), None, None),
            P(("groups", "mp"), None, None, None, None),
            P("groups", None),
            P("groups"),
        ),
        check_vma=False,
    )
```

time: 221 us -> 155 us (0.70)
  Pallas kernels: 149 us -> 118 us
  local copies, waits for them, and re-layouts: 28.6 us -> 13.3 us
  blocking collectives: 15.3 us -> 0 us
  other arithmetic: 24.6 us -> 18.5 us
    pallas_call x4 -> x3, Pallas kernels: 70 us -> 49.2 us  [exchange(): pl.pallas_call(functools.partial(exchange_kernel, n, len(xs)), out_shape=...]
    mul x2 -> x0, local copies, waits for them, and re-layouts: 16.8 us -> none  [the longest x1 8.4 us: shards(): kron = jnp.kron(pointwise_weight, eye)]
    all_gather x1 -> x0, blocking collectives: 15.3 us -> none  [shards(): total = jnp.sum(lax.all_gather(sums, 'mp'), axis=0) * factor]
    pallas_call x3, Pallas kernels: 78.6 us -> 69.1 us  [call(): pl.pallas_call(functools.partial(kernel, rows), out_shape=outs, in_specs=...]
    mul x2 -> x1, other arithmetic: 3.68 us -> 0.01 us  [shards(): total = total.reshape(C, LANES) * factor]
where the time goes in v2:
time: 155 us
  Pallas kernels  118 us (76%)
  other arithmetic  18.5 us (12%)
  local copies, waits for them, and re-layouts  13.3 us (9%)
  matrix products  3.75 us (2%)
    pallas_call x3, Pallas kernels, call(): pl.pallas_call(functools.partial(kernel, rows), out_shape=outs, in_specs=...  69.1 us
    pallas_call x3, Pallas kernels, exchange(): pl.pallas_call(functools.partial(exchange_kernel, n, len(xs)), out_shape=...  49.2 us
    reduce_sum x1, other arithmetic, shards(): u_r = jnp.sum(s_r * w_r - s_i * w_i, axis=2)  5.54 us
    reduce_sum x1, other arithmetic, shards(): m_r = jnp.sum(e_r * w_r + e_i * w_i, axis=3)  4.66 us
    another operation x1, other arithmetic, shards(): jnp.stack([s_r * e_r + s_i * e_i, s_r * e_i - s_i * e_r], axis=1)  4.47 us
    unnamed x19, local copies, waits for them, and re-layouts  4.02 us

profile of v2, /device:TPU:15, one launch (start us, length us, event | category | flops | bytes accessed | tf_op | source)
XLA Modules:
  0.0 154.9 jit_solution(14760273491387132224)
XLA Ops:
  0.6 20.1 %analysis.1 = f32[16,8,1024]{2,1,0:T(8,128)} custom-call(bf16[32,1024,128]{2,1,0:T(8,128)(2,1)} %bitcast.98, bf16[256,1024]{1,0:T(8,128)(2,1)} %constant.20.clone.refs_1_.fy, bf16[2048,256]{1,0:T(8,128)(2,1)} %constant.22.clone.refs_2_), custom_call_target="tpu_custom_call" | custom-call | tf_op jit(solution)/shard_map/analysis/pallas_call | solution.py:346
  20.8 1.4 fusion.10
  22.2 0.4 reshape.209
  22.7 0.1 copy.50
  22.8 0.1 copy.48
  23.0 5.5 %fusion.1 = (f32[16,16,32]{2,1,0:T(8,128)S(1)}, f32[16,16,32]{2,1,0:T(8,128)S(1)}) fusion(f32[16,2,16,32,32]{4,3,2,1,0:T(8,128)} %param.15, f32[16,16,32]{2,1,0:T(8,128)S(1)} %bitcast.102, f32[16,16,32]{2,1,0:T(8,128)S(1)} %bitcast.104), kind=kLoop, calls=%fused_computation.6 | loop fusion | flops 2080768 | bytes 2228224 | tf_op jit(solution)/shard_map/reduce_sum | solution.py:423
  28.5 0.1 copy.52
  28.6 0.1 copy.51
  28.8 0.5 copy.53
  29.4 0.3 reshape.210
  29.7 1.0 fusion.18
  30.6 0.9 reshape.211
  31.5 0.8 fusion.17
  32.4 0.1 add.59
  32.4 0.1 sub.59
  32.5 0.5 pad_maximum_fusion.1
  33.0 0.4 reshape.212.refs_0_
  33.4 15.5 %exchange2.1 = f32[16,8,1024]{2,1,0:T(8,128)S(1)} custom-call(f32[16,8,1024]{2,1,0:T(8,128)S(1)} %reshape.212.refs_0_), custom_call_target="tpu_custom_call" | custom-call | tf_op jit(solution)/shard_map/exchange2/pallas_call | solution.py:326
  49.0 0.8 copy-done
  49.8 0.1 broadcast_in_dim.4
  49.9 0.9 broadcast_in_dim_reshape.4.bias
  50.7 34.0 %middle.1 = (bf16[32,1024,128]{2,1,0:T(8,128)(2,1)}, f32[128,1024]{1,0:T(8,128)}, f32[32,128]{1,0:T(8,128)}) custom-call(bf16[32,1024,128]{2,1,0:T(8,128)(2,1)} %bitcast.99, bf16[32,1024,128]{2,1,0:T(8,128)(2,1)} %bitcast.100, f32[128,1024]{1,0:T(8,128)} %bitcast.94, bf16[32,32]{1,0:T(8,128)(2,1)} %weight.1, f32[512,1]{1,0:T(8,128)} %broadcast_in_dim_reshape.4.bias, ...), custom_call_target="tpu_custom_call" | custom-call | tf_op jit(solution)/shard_map/middle/pallas_call | solution.py:346
  84.7 1.0 copy-done.2
  85.7 0.7 copy-done.3
  86.5 16.7 %exchange3.1 = (f32[16,8,1024]{2,1,0:T(8,128)S(1)}, f32[16,2,128]{2,1,0:T(2,128)S(1)}) custom-call(f32[16,8,1024]{2,1,0:T(8,128)S(1)} %bitcast.96, f32[16,2,128]{2,1,0:T(2,128)S(1)} %bitcast.97), custom_call_target="tpu_custom_call" | custom-call | tf_op jit(solution)/shard_map/exchange3/pallas_call | solution.py:326
  103.2 0.4 fusion.8
  103.6 0.4 reshape.217
  104.0 0.1 copy.60
  104.2 0.1 copy.59
  104.3 4.7 %fusion.5 = (f32[16,16,32]{2,1,0:T(8,128)S(1)}, f32[16,16,32]{2,1,0:T(8,128)S(1)}) fusion(f32[16,2,16,32,32]{4,3,2,1,0:T(8,128)} %param.15, f32[16,16,32]{2,1,0:T(8,128)S(1)} %bitcast.106, f32[16,16,32]{2,1,0:T(8,128)S(1)} %bitcast.108), kind=kLoop, calls=%fused_computation.10 | loop fusion | flops 2080768 | bytes 2228224 | tf_op jit(solution)/shard_map/reduce_sum | solution.py:452
  109.0 0.1 copy.62
  109.1 0.1 copy.61
  109.3 0.5 copy.63
  109.8 0.3 reshape.218
  110.1 1.0 fusion.19
  111.1 0.9 reshape.219
  112.0 0.8 fusion.16
  112.8 0.1 add.64
  112.9 0.1 sub.64
  113.0 0.5 pad_maximum_fusion.2
  113.5 0.4 reshape.220.refs_0_
  113.9 17.0 %exchange4.1 = (f32[16,8,1024]{2,1,0:T(8,128)S(1)}, f32[16,2,128]{2,1,0:T(2,128)S(1)}) custom-call(f32[16,8,1024]{2,1,0:T(8,128)S(1)} %reshape.220.refs_0_, f32[16,2,128]{2,1,0:T(2,128)S(1)} %broadcast_in_dim.5.refs_1_), custom_call_target="tpu_custom_call" | custom-call | tf_op jit(solution)/shard_map/exchange4/pallas_call | solution.py:326
  130.9 0.8 copy-done.1
  131.7 0.7 copy.68
  132.4 15.0 %synthesis.1 = bf16[32,1024,128]{2,1,0:T(8,128)(2,1)} custom-call(bf16[32,1024,128]{2,1,0:T(8,128)(2,1)} %get-tuple-element.11.pg_hbm, f32[128,1024]{1,0:T(8,128)} %bitcast.95, bf16[32,32]{1,0:T(8,128)(2,1)} %bitcast.128, bf16[256,2048]{1,0:T(8,128)(2,1)} %constant.24.clone.gz, bf16[1024,256]{1,0:T(8,128)(2,1)} %constant.21.clone.gy), custom_call_target="tpu_custom_call" | custom-call | tf_op jit(solution)/shard_map/synthesis/pallas_call | solution.py:346
  147.4 2.3 %multiply_add_fusion = (f32[16,1,16,32,32]{4,3,2,1,0:T(8,128)S(1)}, f32[16,1,16,32,32]{4,3,2,1,0:T(8,128)S(1)}) fusion(f32[16,16,32]{2,1,0:T(8,128)S(1)} %bitcast.107, f32[16,16,32]{2,1,0:T(8,128)S(1)} %bitcast.103, f32[16,16,32]{2,1,0:T(8,128)S(1)} %bitcast.109, f32[16,16,32]{2,1,0:T(8,128)S(1)} %bitcast.105), kind=kLoop, calls=%fused_computation.18 | loop fusion | flops 1572864 | bytes 2228224 | tf_op jit(solution)/shard_map/add | solution.py:456
  149.7 4.5 %pad_maximum_fusion = f32[16,2,16,32,32]{4,3,2,1,0:T(8,128)} fusion(f32[16,1,16,32,32]{4,3,2,1,0:T(8,128)S(1)} %get-tuple-element.35, f32[16,1,16,32,32]{4,3,2,1,0:T(8,128)S(1)} %get-tuple-element.34), kind=kLoop, calls=%fused_computation | loop fusion | flops 524288 | bytes 4194304 | tf_op jit(solution)/shard_map/stack | solution.py:456
  154.2 0.7 slice_reduce_fusion
  (21 shorter events, 0.3 us)
Async XLA Ops:
  0.6 20.2 %copy-start.6 = (f32[32,128]{1,0:T(8,128)S(1)}, f32[32,128]{1,0:T(8,128)}, u32[]{:S(2)}) copy-start(f32[32,128]{1,0:T(8,128)} %constant.26.clone) | copy-start | bytes 49156
  23.0 6.7 %copy-start.4 = (f32[256,16]{1,0:T(8,128)S(1)}, f32[256,16]{1,0:T(8,128)}, u32[]{:S(2)}) copy-start(f32[256,16]{1,0:T(8,128)} %constant.27.clone) | copy-start | bytes 49156
  30.6 19.2 %copy-start.8 = (f32[32]{0:T(128)S(1)}, f32[32]{0:T(128)}, u32[]{:S(2)}) copy-start(f32[32]{0:T(128)} %param.17) | copy-start | bytes 388
  49.0 0.8 copy-start
  84.7 1.0 copy-start.2
  85.7 0.7 copy-start.3
  111.1 20.6 %copy-start.7 = (bf16[32,32]{1,0:T(8,128)(2,1)S(1)}, bf16[32,32]{1,0:T(8,128)(2,1)}, u32[]{:S(2)}) copy-start(bf16[32,32]{1,0:T(8,128)(2,1)} %weight.1) | copy-start | bytes 6148
  130.9 0.8 copy-start.1
  154.2 0.7 copy-start.5

commit v3 on v2

--- a/solution.py
+++ b/solution.py
@@ -60,7 +60,9 @@
     gz_w = (np.einsum("rqzk,ab,k->rakbqz", back, oct_eye, wz)).reshape(gz.shape)
     fx = np.concatenate([xc.T, xs.T], 0).astype(np.float32)
     gx = np.concatenate([xc, xs], 0).astype(np.float32)
-    return low(fy), low(gy), low(fz), low(fz_w), low(gz), low(gz_w), fx, gx
+    fx2 = np.block([[xc.T, xs.T], [-xs.T, xc.T]]).astype(np.float32)
+    gx2 = np.block([[xc, -xs], [xs, xc]]).astype(np.float32)
+    return low(fy), low(gy), low(fz), low(fz_w), low(gz), low(gz_w), fx, gx, fx2, gx2
 
 
 def dot(a, b):
@@ -137,50 +139,79 @@
     )
 
 
-def analysis_kernel(rows, n, feat_hbm, fy, fz, dst, feat, src, load, send, recv, own):
+def send_half(n, half, src, dst, send, recv, own):
     me = lax.axis_index("mp")
+    wide = GLANES * GROUPS // 2
+    lanes = pl.ds(half * wide, wide)
+
+    @pl.loop(1, n)
+    def _(s):
+        peer = lax.rem(me + s, n)
+        remote(
+            src.at[peer, :, lanes],
+            dst.at[me, :, lanes],
+            send.at[half, peer],
+            recv.at[half, me],
+            peer,
+        ).start()
+
+    mine = pltpu.make_async_copy(src.at[me, :, lanes], dst.at[me, :, lanes], own.at[half])
+    mine.start()
+    return mine
+
+
+def wait_half(n, half, src, dst, send, recv):
+    me = lax.axis_index("mp")
+    wide = GLANES * GROUPS // 2
+    lanes = pl.ds(half * wide, wide)
+
+    @pl.loop(1, n)
+    def _(s):
+        peer = lax.rem(me + s, n)
+        both = remote(
+            src.at[peer, :, lanes],
+            dst.at[peer, :, lanes],
+            send.at[half, peer],
+            recv.at[half, peer],
+            peer,
+        )
+        both.wait_recv()
+        both.wait_send()
+
+
+def spread_out(rows, n, field, fy, fz, fx2, spec, src, dst, send, recv, own, ready):
+    mine = []
+    for half in range(2):
+        for g in range(half * GROUPS // 2, (half + 1) * GROUPS // 2):
+            ready(g)
+            res = forward_group(field, g, fy, fz, KY * rows)
+            src[:, :, g * GLANES : (g + 1) * GLANES] = res.reshape(KY, rows, GLANES)
+        if half == 0:
+            pl.semaphore_wait(pltpu.get_barrier_semaphore(), n - 1)
+        mine.append(send_half(n, half, src, dst, send, recv, own))
+    each = GLANES // 2
+    for half in range(2):
+        mine[half].wait()
+        wait_half(n, half, src, dst, send, recv)
+        for g in range(half * GROUPS // 2, (half + 1) * GROUPS // 2):
+            pair = [
+                dst[:, :, g * GLANES + r * each : g * GLANES + (r + 1) * each].reshape(NX, each)
+                for r in range(2)
+            ]
+            spec[:, g * each : (g + 1) * each] = jnp.dot(
+                fx2[...],
+                jnp.concatenate(pair, axis=0),
+                precision=precise,
+                preferred_element_type=F32,
+            )
+
+
+def analysis_kernel(rows, n, feat_hbm, fy, fz, fx2, spec, feat, load, src, dst, send, recv, own):
     greet(n)
     loads = load_groups(feat_hbm, feat, load)
-    mine = []
-    wide = GLANES * GROUPS // 2
-    for half in range(2):
-        for g in range(half * GROUPS // 2, (half + 1) * GROUPS // 2):
-            loads[g].wait()
-            res = forward_group(feat, g, fy, fz, KY * rows)
-            src[:, :, g * GLANES : (g + 1) * GLANES] = res.reshape(KY, rows, GLANES)
-        lanes = pl.ds(half * wide, wide)
-        if half == 0:
-            pl.semaphore_wait(pltpu.get_barrier_semaphore(), n - 1)
-
-        @pl.loop(1, n)
-        def _(s):
-            peer = lax.rem(me + s, n)
-            remote(
-                src.at[peer, :, lanes],
-                dst.at[me, :, lanes],
-                send.at[half, peer],
-                recv.at[half, me],
-                peer,
-            ).start()
-
-        mine.append(pltpu.make_async_copy(src.at[me, :, lanes], dst.at[me, :, lanes], own.at[half]))
-        mine[-1].start()
-    for half in range(2):
-        lanes = pl.ds(half * wide, wide)
-        mine[half].wait()
-
-        @pl.loop(1, n)
-        def _(s):
-            peer = lax.rem(me + s, n)
-            both = remote(
-                src.at[peer, :, lanes],
-                dst.at[peer, :, lanes],
-                send.at[half, peer],
-                recv.at[half, peer],
-                peer,
-            )
-            both.wait_recv()
-            both.wait_send()
+    spread_out(
+        rows, n, feat, fy, fz, fx2, spec, src, dst, send, recv, own, lambda g: loads[g].wait()
+    )
 
 
 def forward_kernel(rows, feat, fy, fz, out):
@@ -213,9 +244,11 @@
 
 
 def middle_kernel(
-    rows, feat_hbm, cot_hbm, modes, weight, bias, gz, gy, fy, fz, pg_hbm, part, sums,
-    field, acc, bacc, kron, feat, cot, pg, fsem, csem, psem,
+    rows, n, feat_hbm, cot_hbm, modes, weight, bias, gz, gy, fy, fz, fx2, pg_hbm, part, sums,
+    field, acc, bacc, kron, feat, cot, pg, fsem, csem, psem, *net,
 ):
+    if net:
+        greet(n)
     loads = load_groups(feat_hbm, feat, fsem) + load_groups(cot_hbm, cot, csem)
     kron[...] = widen(weight[...])
     acc[...] = jnp.zeros_like(acc)
@@ -245,14 +278,14 @@
 
     save = pltpu.make_async_copy(pg, pg_hbm, psem)
     save.start()
-    n = C * TILE
-    ri = lax.broadcasted_iota(jnp.int32, (n, n), 0)
-    ci = lax.broadcasted_iota(jnp.int32, (n, n), 1)
+    size = C * TILE
+    ri = lax.broadcasted_iota(jnp.int32, (size, size), 0)
+    ci = lax.broadcasted_iota(jnp.int32, (size, size), 1)
     masked = jnp.where(ri % TILE == ci % TILE, acc[...], 0.0)
-    rows_sum = jnp.sum(masked.reshape(C, TILE, n), axis=1)
+    rows_sum = jnp.sum(masked.reshape(C, TILE, size), axis=1)
     fold = jnp.where(
-        lax.broadcasted_iota(jnp.int32, (n, LANES), 0) // TILE
-        == lax.broadcasted_iota(jnp.int32, (n, LANES), 1),
+        lax.broadcasted_iota(jnp.int32, (size, LANES), 0) // TILE
+        == lax.broadcasted_iota(jnp.int32, (size, LANES), 1),
         1.0,
         0.0,
     ).astype(F32)
@@ -260,7 +293,10 @@
     by_row = jnp.sum(bacc[...].reshape(C, TILE, NZ), axis=1)
     lane = lax.broadcasted_iota(jnp.int32, (C, LANES), 1)
     sums[...] = pw + jnp.where(lane == C, jnp.sum(by_row, axis=1, keepdims=True), 0.0)
-    plain_forward(pg, fy, fz, part, KY * rows)
+    if net:
+        spread_out(rows, n, pg, fy, fz, fx2, part, *net, lambda g: None)
+    else:
+        plain_forward(pg, fy, fz, part, KY * rows)
     save.wait()
 
 
@@ -291,11 +327,22 @@
         copy.wait()
 
 
-def exchange_kernel(n, arrays, *refs):
-    srcs, dsts = refs[:arrays], refs[arrays : 2 * arrays]
-    send, recv, own = refs[2 * arrays :]
+def exchange_kernel(n, arrays, spread, *refs):
     me = lax.axis_index("mp")
     greet(n)
+    srcs = refs[:arrays]
+    if spread:
+        table, refs, lines = refs[arrays], refs[:arrays] + refs[arrays + 1 : -1], refs[-1]
+        each = GLANES // 2
+        for g in range(GROUPS):
+            part = srcs[0][:, g * each : (g + 1) * each]
+            both = jnp.dot(table[...], part, precision=precise, preferred_element_type=F32)
+            for r in range(2):
+                at = g * GLANES + r * each
+                lines[:, :, at : at + each] = both[r * NX : (r + 1) * NX].reshape(n, NX // n, each)
+        srcs = (lines, *srcs[1:])
+    dsts = refs[arrays : 2 * arrays]
+    send, recv, own = refs[2 * arrays :]
     pl.semaphore_wait(pltpu.get_barrier_semaphore(), n - 1)
 
     @pl.loop(1, n)
@@ -322,22 +369,28 @@
             both.wait_send()
 
 
-def exchange(xs, n, cid):
+def exchange(xs, n, cid, table=None):
+    shapes = [jax.ShapeDtypeStruct(x.shape, x.dtype) for x in xs]
+    extra = []
+    if table is not None:
+        shapes[0] = jax.ShapeDtypeStruct((n, NX // n, 2 * C * KZ), F32)
+        extra = [table]
     return pl.pallas_call(
-        functools.partial(exchange_kernel, n, len(xs)),
-        out_shape=[jax.ShapeDtypeStruct(x.shape, x.dtype) for x in xs],
-        in_specs=[VMEM] * len(xs),
+        functools.partial(exchange_kernel, n, len(xs), table is not None),
+        out_shape=shapes,
+        in_specs=[VMEM] * (len(xs) + len(extra)),
         out_specs=[VMEM] * len(xs),
         scratch_shapes=[
             pltpu.SemaphoreType.DMA((len(xs), n)),
             pltpu.SemaphoreType.DMA((len(xs), n)),
             pltpu.SemaphoreType.DMA((len(xs),)),
-        ],
+        ]
+        + [pltpu.VMEM(shapes[0].shape, F32)] * len(extra),
         compiler_params=pltpu.CompilerParams(
             collective_id=cid, has_side_effects=True, vmem_limit_bytes=16 << 20
         ),
         name=f"exchange{cid}",
-    )(*xs)
+    )(*xs, *extra)
 
 
 def call(kernel, rows, outs, scratch, args, name, far=(), far_out=(), cid=None):
@@ -387,10 +440,19 @@
     return lines.reshape(n, rows, -1)
 
 
+def split_modes(spec):
+    v = jnp.transpose(spec.reshape(2, KX, C, KZ), (0, 3, 1, 2))
+    return v[0], v[1]
+
+
+def join_modes(real, imag):
+    return jnp.transpose(jnp.stack([real, imag]), (0, 2, 3, 1)).reshape(2 * KX, C * KZ)
+
+
 def shards(features, cotangent, spectral_weight, pointwise_weight, biases):
     n = lax.axis_size("mp")
     rows = NX // n
-    fy, gy, fz, fz_w, gz, gz_w, fx, gx = [jnp.asarray(t) for t in tables(rows)]
+    fy, gy, fz, fz_w, gz, gz_w, fx, gx, fx2, gx2 = [jnp.asarray(t) for t in tables(rows)]
     cells = rows * NY
     feat = features.reshape(C, cells, NZ)
     cot = cotangent.reshape(C, cells, NZ)
@@ -400,31 +462,37 @@
     field = pltpu.VMEM((C, cells, NZ), F32)
     block = pltpu.VMEM((C, cells, NZ), BF)
     wide = C * TILE
-    sems = pltpu.SemaphoreType.DMA((GROUPS,))
-    if n == KY:
-        blocks = jax.ShapeDtypeStruct((n, rows, 2 * C * KZ), F32)
-        dma = pltpu.SemaphoreType.DMA
-        got = call(
+    dma = pltpu.SemaphoreType.DMA
+    sems = dma((GROUPS,))
+    fused = n == KY
+    lines = pltpu.VMEM((n, rows, 2 * C * KZ), F32)
+    net = [lines, lines, dma((2, n)), dma((2, n)), dma((2,))] if fused else []
+    if fused:
+        spread = jax.ShapeDtypeStruct((2 * KX, C * KZ), F32)
+        spec = call(
             lambda r, *refs: analysis_kernel(r, n, *refs),
             rows,
-            [blocks],
-            [block, pltpu.VMEM(blocks.shape, F32), sems, dma((2, n)), dma((2, n)), dma((2,))],
-            (feat, fy, fz),
+            [spread],
+            [block, sems, *net],
+            (feat, fy, fz, fx2),
             "analysis",
             far=(0,),
             cid=1,
         )[0]
+        v_r, v_i = split_modes(spec)
     else:
         part = call(forward_kernel, rows, [spread], [], (feat, fy, fz), "analysis")[0]
-        got = exchange([owner_blocks(part, n, rows)], n, 1)[0]
-    v_r, v_i = lines_forward(got, fx)
+        v_r, v_i = lines_forward(exchange([owner_blocks(part, n, rows)], n, 1)[0], fx)
     w_r, w_i = spectral_weight[:, 0], spectral_weight[:, 1]
     s_r, s_i = v_r[..., None], v_i[..., None]
     u_r = jnp.sum(s_r * w_r - s_i * w_i, axis=2)
     u_i = jnp.sum(s_r * w_i + s_i * w_r, axis=2)
-    modes = plane_blocks(exchange([lines_back(u_r, u_i, gx, n, rows)], n, 2)[0], n, rows)
+    if fused:
+        modes = exchange([join_modes(u_r, u_i)], n, 2, gx2)[0]
+    else:
+        modes = exchange([lines_back(u_r, u_i, gx, n, rows)], n, 2)[0]
     pg, dpart, sums = call(
-        middle_kernel,
+        lambda r, *refs: middle_kernel(r, n, *refs),
         rows,
         [whole, spread, jax.ShapeDtypeStruct((C, LANES), F32)],
         [
@@ -437,23 +505,34 @@
             block,
             sems,
             sems,
-            pltpu.SemaphoreType.DMA,
+            dma,
+            *net,
         ],
-        (feat, cot, modes, pointwise_weight, bias, gz_w, gy, fy, fz_w),
+        (feat, cot, plane_blocks(modes, n, rows), pointwise_weight, bias, gz_w, gy, fy, fz_w, fx2),
         "middle",
         far=(0, 1),
         far_out=(0,),
+        cid=3 if fused else None,
     )
-    got, got_sums = exchange(
-        [owner_blocks(dpart, n, rows), sums.reshape(n, C // n, LANES)], n, 3
-    )
-    d_r, d_i = lines_forward(got, fx)
+    if fused:
+        d_r, d_i = split_modes(dpart)
+    else:
+        d_r, d_i = lines_forward(exchange([owner_blocks(dpart, n, rows)], n, 3)[0], fx)
     e_r, e_i = d_r[:, :, None, :], d_i[:, :, None, :]
     m_r = jnp.sum(e_r * w_r + e_i * w_i, axis=3)
     m_i = jnp.sum(e_i * w_r - e_r * w_i, axis=3)
-    mine = jnp.broadcast_to(jnp.sum(got_sums, axis=0), (n, C // n, LANES))
-    back, total = exchange([lines_back(m_r, m_i, gx, n, rows), mine], n, 4)
-    spectral_grad = jnp.stack([s_r * e_r + s_i * e_i, s_r * e_i - s_i * e_r], axis=1)
+    packed = jnp.concatenate(
+        [sums[:, :C].reshape(-1, LANES), jnp.pad(sums[:, C], (0, LANES - C))[None]], axis=0
+    )
+    mine = jnp.broadcast_to(packed, (n, *packed.shape))
+    if fused:
+        back, every = exchange([join_modes(m_r, m_i), mine], n, 4, gx2)
+    else:
+        back, every = exchange([lines_back(m_r, m_i, gx, n, rows), mine], n, 4)
+    total = jnp.sum(every, axis=0)
+    first = jnp.stack([v_r, -v_i], axis=1)[..., None]
+    second = jnp.stack([v_i, v_r], axis=1)[..., None]
+    spectral_grad = first * e_r[:, None] + second * e_i[:, None]
     grad = call(
         last_kernel,
         rows,
@@ -465,8 +544,8 @@
         far_out=(0,),
     )[0]
     factor = float(NX * NY * NZ) ** (-0.5)
-    total = total.reshape(C, LANES) * factor
-    return (grad.reshape(features.shape), spectral_grad, total[:, :C], total[:, C])
+    total = total * factor
+    return (grad.reshape(features.shape), spectral_grad, total[:-1].reshape(C, C), total[-1, :C])
 
 
 def solution(mesh):

time: 155 us -> 144 us (0.929)
  Pallas kernels: 118 us -> 114 us
  matrix products: 3.75 us -> 0 us
    pallas_call x3 -> x2, Pallas kernels: 49.2 us -> 34.8 us  [exchange(): pl.pallas_call(functools.partial(exchange_kernel, n, len(xs), table is no...]
    pallas_call x3, Pallas kernels: 69.1 us -> 79 us  [call(): pl.pallas_call(functools.partial(kernel, rows), out_shape=outs, in_specs=...]
    another operation x3 -> x1, other arithmetic: 5.42 us -> 0.13 us  [shards(): first = jnp.stack([v_r, -v_i], axis=1)[..., None]]
    add x5 -> x1, other arithmetic: 2.6 us -> 6.92 us  [shards(): spectral_grad = first * e_r[:, None] + second * e_i[:, None]]
    dot_general x4 -> x0, matrix products: 3.75 us -> none  [the longest x2 1.92 us: lines_back(): jnp.einsum('qa,al->ql', gx, u, precision=precise)]
    unnamed x19 -> x7, local copies, waits for them, and re-layouts: 4.02 us -> 2.96 us
    reshape x8 -> x6, local copies, waits for them, and re-layouts: 3.87 us -> 4.09 us  [the longest x2 2.08 us: split_modes(): v = jnp.transpose(spec.reshape(2, KX, C, KZ), (0, 3, 1, 2))]
where the time goes in v3:
time: 144 us
  Pallas kernels  114 us (79%)
  other arithmetic  17.3 us (12%)
  local copies, waits for them, and re-layouts  11.8 us (8%)
    pallas_call x3, Pallas kernels, call(): pl.pallas_call(functools.partial(kernel, rows), out_shape=outs, in_specs=...  79 us
    pallas_call x2, Pallas kernels, exchange(): pl.pallas_call(functools.partial(exchange_kernel, n, len(xs), table is no...  34.8 us
    add x1, other arithmetic, shards(): spectral_grad = first * e_r[:, None] + second * e_i[:, None]  6.92 us
    reduce_sum x1, other arithmetic, shards(): u_r = jnp.sum(s_r * w_r - s_i * w_i, axis=2)  5.51 us
    reduce_sum x1, other arithmetic, shards(): m_r = jnp.sum(e_r * w_r + e_i * w_i, axis=3)  4.66 us
    unnamed x7, local copies, waits for them, and re-layouts  2.96 us

profile of v3, /device:TPU:15, one launch (start us, length us, event | category | flops | bytes accessed | tf_op | source)
XLA Modules:
  0.0 143.8 jit_solution(4861514959181300141)
XLA Ops:
  0.6 1.4 copy.46
  2.0 0.7 broadcast_in_dim.11
  2.7 20.2 %analysis.1 = f32[32,512]{1,0:T(8,128)} custom-call(bf16[32,1024,128]{2,1,0:T(8,128)(2,1)} %bitcast.77, bf16[256,1024]{1,0:T(8,128)(2,1)} %constant.22.clone.refs_1_.refs_7_, bf16[2048,256]{1,0:T(8,128)(2,1)} %constant.24.clone.refs_2_, f32[32,256]{1,0:T(8,128)} %constant.28.clone.refs_3_.refs_9_), custom_call_target="tpu_custom_call" | custom-call | tf_op jit(solution)/shard_map/analysis/pallas_call | solution.py:399
  22.9 0.9 broadcast_in_dim_reshape.4.refs_4_
  23.8 1.0 reshape.61
  24.8 0.1 slice_bitcast_fusion.2
  25.0 0.1 copy.40
  25.1 0.1 copy.38
  25.2 5.5 %fusion.1 = (f32[16,16,32]{2,1,0:T(8,128)S(1)}, f32[16,16,32]{2,1,0:T(8,128)S(1)}) fusion(f32[16,2,16,32,32]{4,3,2,1,0:T(8,128)} %param.15, f32[16,16,32]{2,1,0:T(8,128)S(1)} %copy.40, f32[16,16,32]{2,1,0:T(8,128)S(1)} %copy.38), kind=kLoop, calls=%fused_computation.6 | loop fusion | flops 2080768 | bytes 2228224 | tf_op jit(solution)/shard_map/reduce_sum | solution.py:488
  30.8 0.0 copy-start.2
  30.8 0.2 copy.41
  31.0 0.3 reshape.62.refs_0_
  31.3 0.1 pad_maximum_fusion
  31.5 0.3 copy.47
  31.7 0.3 copy.49
  32.0 0.0 copy-done.2
  32.0 15.5 %exchange2.1 = f32[16,8,1024]{2,1,0:T(8,128)S(1)} custom-call(f32[32,512]{1,0:T(8,128)S(1)} %reshape.62.refs_0_, f32[256,32]{1,0:T(8,128)S(1)} %copy-done.2), custom_call_target="tpu_custom_call" | custom-call | tf_op jit(solution)/shard_map/exchange2/pallas_call | solution.py:378
  47.6 0.0 copy-start
  47.6 0.8 copy-done
  48.4 43.9 %middle.1 = (bf16[32,1024,128]{2,1,0:T(8,128)(2,1)}, f32[32,512]{1,0:T(8,128)}, f32[32,128]{1,0:T(8,128)}) custom-call(bf16[32,1024,128]{2,1,0:T(8,128)(2,1)} %bitcast.78, bf16[32,1024,128]{2,1,0:T(8,128)(2,1)} %bitcast.79, f32[128,1024]{1,0:T(8,128)} %bitcast.75, bf16[32,32]{1,0:T(8,128)(2,1)} %refs_3_.2, f32[512,1]{1,0:T(8,128)} %broadcast_in_dim_reshape.4.refs_4_, ...), custom_call_target="tpu_custom_call" | custom-call | tf_op jit(solution)/shard_map/middle/pallas_call | solution.py:399
  92.2 0.9 slice_reduce_fusion
  93.1 0.8 reshape.66
  94.0 1.0 reshape.64
  95.1 0.1 copy.43
  95.2 0.1 copy.44
  95.3 4.7 %fusion.5 = (f32[16,16,32]{2,1,0:T(8,128)S(1)}, f32[16,16,32]{2,1,0:T(8,128)S(1)}) fusion(f32[16,2,16,32,32]{4,3,2,1,0:T(8,128)} %param.15, f32[16,16,32]{2,1,0:T(8,128)S(1)} %copy.44, f32[16,16,32]{2,1,0:T(8,128)S(1)} %copy.43), kind=kLoop, calls=%fused_computation.10 | loop fusion | flops 2080768 | bytes 2228224 | tf_op jit(solution)/shard_map/reduce_sum | solution.py:522
  100.0 0.2 copy.45
  100.3 0.3 reshape.65.refs_0_
  100.5 19.3 %exchange4.1 = (f32[16,8,1024]{2,1,0:T(8,128)S(1)}, f32[16,9,128]{2,1,0:T(8,128)S(1)}) custom-call(f32[32,512]{1,0:T(8,128)S(1)} %reshape.65.refs_0_, f32[16,9,128]{2,1,0:T(8,128)S(1)} %broadcast_in_dim.13.refs_1_, f32[256,32]{1,0:T(8,128)S(1)} %copy-done.2), custom_call_target="tpu_custom_call" | custom-call | tf_op jit(solution)/shard_map/exchange4/pallas_call | solution.py:378
  119.8 0.0 copy-start.1
  119.8 0.8 copy-done.1
  120.6 15.0 %synthesis.1 = bf16[32,1024,128]{2,1,0:T(8,128)(2,1)} custom-call(bf16[32,1024,128]{2,1,0:T(8,128)(2,1)} %get-tuple-element.9.pg_hbm, f32[128,1024]{1,0:T(8,128)} %bitcast.76, bf16[32,32]{1,0:T(8,128)(2,1)} %bitcast.89, bf16[256,2048]{1,0:T(8,128)(2,1)} %constant.26.clone.gz, bf16[1024,256]{1,0:T(8,128)(2,1)} %constant.23.clone.refs_6_.gy), custom_call_target="tpu_custom_call" | custom-call | tf_op jit(solution)/shard_map/synthesis/pallas_call | solution.py:399
  135.7 0.5 slice_bitcast_fusion.6
  136.2 0.7 reshape.69
  136.8 6.9 %multiply_add_fusion = f32[16,2,16,32,32]{4,3,2,1,0:T(8,128)} fusion(f32[16,16,32]{2,1,0:T(8,128)S(1)} %copy.44, f32[16,2,16,32]{3,2,1,0:T(8,128)S(1)} %copy.49, f32[16,16,32]{2,1,0:T(8,128)S(1)} %copy.43, f32[16,2,16,32]{3,2,1,0:T(8,128)S(1)} %copy.47), kind=kLoop, calls=%fused_computation | loop fusion | flops 1572864 | bytes 2293760 | tf_op jit(solution)/shard_map/add | solution.py:535
  (10 shorter events, 0.2 us)
Async XLA Ops:
  30.8 1.2 copy-start.2
  47.6 0.8 copy-start
  119.8 0.8 copy-start.1
